TPU v7x, 512 devices: a whole 4x8x8 slice. The times are simulated.
512 devices in a mesh: space: 64 (over y, z_hi, x), vec: 8 (over z_lo, core).
Axes of the slice: x: 4, y: 8, z: 8 (z_hi: 2, z_lo: 4; z = z_hi * 4 + z_lo), core: 2. Of those that a mesh axis runs over, the one named last changes fastest.
Arguments:
- node_feat: bfloat16 [8192, 256], P('space'), may hold values from -6 to 6
- radial: bfloat16 [131072, 128], P(('space', 'vec')), may hold values from -6 to 6
- edge_src: int32 [131072], P(('space', 'vec')), may hold values from 0 to 127
- edge_dst: int32 [131072], P(('space', 'vec')), may hold values from 0 to 255
- edge_live: int32 [131072], P(('space', 'vec')), may hold values 0 or 1
- w_src: bfloat16 [256, 256], replicated, may hold values from -0.375 to 0.375
- w_dst: bfloat16 [256, 256], replicated, may hold values from -0.375 to 0.375
- w_radial: bfloat16 [128, 256], replicated, may hold values from -0.5 to 0.5
- w_hidden: bfloat16 [2, 256, 256], replicated, may hold values from -0.375 to 0.375
- w_out: bfloat16 [169, 256], replicated, may hold values from -0.01953125 to 0.01953125
- start_vectors: float32 [32, 13, 8192], P('vec', None, 'space'), may hold values from -6 to 6
Outputs:
- pair_blocks: bfloat16 [169, 131072], P(None, ('space', 'vec'))
- filtered: float32 [32, 13, 8192], P('vec', None, 'space')
Inputs may be any that keep to these rules, and one draw needn't show every extreme that they name: `edge_dst`: A value below 128 names an atom of the slot's own domain; a value k of 128 or more names atom k - 128 of the next domain, the first domain following the last.
All inputs are finite; a program needn't handle non-finite values. No bound on the sum of `edge_live` on one device may be relied on, other than what follows from the above.
Results may differ from a plain program's by a relative error of at most 0.0062.
Values may be sent and summed in bfloat16 or wider, within the bound.
A program may use at most 64 MiB of HBM per device.

v0:
```python
import math

import jax
import jax.numpy as jnp
from jax import lax
from jax.sharding import PartitionSpec as P


def shifted(x, axis, by):
    length = lax.axis_size(axis)
    return lax.ppermute(x, axis, [(i, (i + by) % length) for i in range(length)])


def apply_pairs(blocks, sources, targets, vectors):
    at_targets = jnp.take(vectors, targets, axis=2)
    at_sources = jnp.take(vectors, sources, axis=2)
    to_first = jnp.einsum("abe,vbe->vae", blocks, at_targets, precision=lax.Precision.HIGHEST)
    to_second = jnp.einsum("bae,vbe->vae", blocks, at_sources, precision=lax.Precision.HIGHEST)
    result = jnp.zeros(vectors.shape, jnp.float32)
    result = result.at[:, :, sources].add(to_first)
    return result.at[:, :, targets].add(to_second)


def on_device(
    node_feat,
    radial,
    edge_src,
    edge_dst,
    edge_live,
    w_src,
    w_dst,
    w_radial,
    w_hidden,
    w_out,
    start_vectors,
):
    atom_count = node_feat.shape[0]
    ghost = shifted(node_feat, "space", -1)
    extended = jnp.concatenate([node_feat, ghost], 0)
    proj_src = jnp.dot(node_feat, w_src, preferred_element_type=jnp.float32)
    proj_dst = jnp.dot(extended, w_dst, preferred_element_type=jnp.float32)
    pre = (
        proj_src[edge_src]
        + proj_dst[edge_dst]
        + jnp.dot(radial, w_radial, preferred_element_type=jnp.float32)
    )
    hidden = jax.nn.silu(pre).astype(jnp.bfloat16)
    for layer in range(w_hidden.shape[0]):
        update = jax.nn.silu(jnp.dot(hidden, w_hidden[layer], preferred_element_type=jnp.float32))
        hidden = (hidden.astype(jnp.float32) + update).astype(jnp.bfloat16)
    raw = lax.dot_general(
        w_out, hidden, (((1,), (1,)), ((), ())), preferred_element_type=jnp.float32
    )
    pair_blocks = (raw * edge_live.astype(jnp.float32)[None, :]).astype(jnp.bfloat16)
    orbitals = math.isqrt(w_out.shape[0])
    pair_lists = jnp.stack([edge_src, edge_dst])
    blocks = pair_blocks.astype(jnp.float32).reshape(orbitals, orbitals, -1)

    def operator(vectors):
        every = lax.all_gather(vectors, "vec", axis=0, tiled=True)
        ghost_all = shifted(every.astype(jnp.bfloat16), "space", -1).astype(every.dtype)
        joined = jnp.concatenate([every, ghost_all], 2)
        result_ext = apply_pairs(blocks, pair_lists[0], pair_lists[1], joined)
        back = shifted(result_ext[:, :, atom_count:].astype(jnp.bfloat16), "space", 1).astype(
            jnp.float32
        )
        summed = result_ext[:, :, :atom_count] + back
        return lax.psum_scatter(summed, "vec", scatter_dimension=0, tiled=True)

    first = operator(start_vectors)
    filtered = 2.0 * operator(first) - start_vectors
    return (pair_blocks, filtered)


def solution(mesh):
    in_specs = (
        P("space", None),
        P(("space", "vec"), None),
        P(("space", "vec")),
        P(("space", "vec")),
        P(("space", "vec")),
        P(),
        P(),
        P(),
        P(),
        P(),
        P("vec", None, "space"),
    )
    out_specs = (P(None, ("space", "vec")), P("vec", None, "space"))
    return jax.shard_map(
        on_device, mesh=mesh, in_specs=in_specs, out_specs=out_specs, check_vma=False
    )
```

profile of v0, /device:TPU:1, one launch (start us, length us, event | category | flops | bytes accessed | tf_op | source)
XLA Modules:
  0.0 301.7 jit_solution(2385422538803884936)
XLA Ops:
  7.2 16.7 %collective-permute-start = (bf16[128,256]{1,0:T(8,128)(2,1)}, bf16[128,256]{1,0:T(8,128)(2,1)S(1)}, u32[]{:S(2)}, u32[]{:S(2)}) collective-permute-start(bf16[128,256]{1,0:T(8,128)(2,1)} %param.13), channel_id=1, source_target_pairs={{0,504},{8,0},{16,8},{24,16},{32,24},{40,32},{48,40},{56,48},{64,5... | collective-permute-start | bytes 196616 | tf_op jit(solution)/shard_map/ppermute | solution.py:11
  24.7 15.0 %all_gather.6 = f32[32,13,128]{2,1,0:T(8,128)S(1)} all-gather(f32[4,13,128]{2,1,0:T(8,128)S(1)} %copy.75), channel_id=1, replica_groups=mesh['space'=64,'vec'=8] {'vec'}, dimensions={0}, use_global_device_ids=true | all-gather | bytes 239616 | tf_op jit(solution)/shard_map/all_gather | solution.py:60
  39.8 2.5 collective-permute-start.1
  53.8 2.3 copy.78
  56.1 2.3 gather_fusion.2
  58.4 2.4 gather_fusion.3
  60.8 4.2 %fusion.6 = f32[256,32,13]{1,2,0:T(8,128)} fusion(bf16[13,13,256]{1,0,2:T(8,128)(2,1)S(1)} %copy.79, f32[256,32,13]{1,2,0:T(8,128)} %gather_fusion.2, pred[256]{0:T(512)(128)(4,1)S(1)} %compare_and_fusion), kind=kOutput, calls=%fused_computation.16 | convolution fusion | flops 16719872 | bytes 938752 | tf_op jit(solution)/shard_map/abe,vbe->vae/dot_general | solution.py:17
  65.1 20.3 %scatter_fusion = f32[32,13,256]{0,1,2:T(8,128)S(1)} fusion(f32[32,13,256]{0,1,2:T(8,128)S(1)} %broadcast.20.clone, s32[256]{0:T(256)S(1)} %get-tuple-element.19, f32[256,32,13]{1,2,0:T(8,128)} %fusion.6), kind=kCustom, calls=%fused_computation.6 | custom fusion | flops 106496 | bytes 1278976 | tf_op jit(solution)/shard_map/scatter-add | solution.py:20
  85.4 4.5 %fusion.4 = f32[256,32,13]{1,2,0:T(8,128)} fusion(bf16[13,13,256]{0,1,2:T(8,128)(2,1)} %copy.81, f32[256,32,13]{1,2,0:T(8,128)} %gather_fusion.3, pred[256]{0:T(512)(128)(4,1)S(1)} %compare_and_fusion.1), kind=kOutput, calls=%fused_computation.14 | convolution fusion | flops 16719872 | bytes 938752 | tf_op jit(solution)/shard_map/bae,vbe->vae/dot_general | solution.py:18
  89.9 20.2 %scatter_fusion.1 = f32[32,13,256]{0,1,2:T(8,128)S(1)} fusion(f32[32,13,256]{0,1,2:T(8,128)S(1)} %scatter_fusion, s32[256]{0:T(256)S(1)} %compare_select_fusion.2, f32[256,32,13]{1,2,0:T(8,128)} %fusion.4), kind=kCustom, calls=%fused_computation.7 | custom fusion | flops 106496 | bytes 1278976 | tf_op jit(solution)/shard_map/scatter-add | solution.py:21
  112.4 2.9 collective-permute-start.2
  117.8 8.9 %collective-permute-done.2 = bf16[32,13,128]{2,0,1:T(8,128)(2,1)S(1)} collective-permute-done((bf16[32,13,128]{2,0,1:T(8,128)(2,1)S(1)}, bf16[32,13,128]{2,0,1:T(8,128)(2,1)S(1)}, u32[]{:S(2)}, u32[]{:S(2)}) %collective-permute-start.2) | collective-permute-done | bytes 106528 | tf_op jit(solution)/shard_map/ppermute | solution.py:11
  127.6 30.5 %reduce-scatter.3.cloned.1.call-done = f32[4,13,128]{2,1,0:T(8,128)} async-done(((f32[32,13,128]{2,1,0:T(8,128)}), f32[4,13,128]{2,1,0:T(8,128)}) %reduce-scatter.3.cloned.1.call-update) | async-done | bytes 26640 | tf_op jit(solution)/shard_map/reduce_scatter | solution.py:68
  158.2 17.6 %all_gather.7 = f32[32,13,128]{2,1,0:T(8,128)S(1)} all-gather(f32[4,13,128]{2,1,0:T(8,128)} %reduce-scatter.3.cloned.1.call-done), channel_id=1, replica_groups=mesh['space'=64,'vec'=8] {'vec'}, dimensions={0}, use_global_device_ids=true | all-gather | bytes 239616 | tf_op jit(solution)/shard_map/all_gather | solution.py:60
  175.8 9.7 %collective-permute-start.3 = (bf16[32,13,128]{2,0,1:T(8,128)(2,1)S(1)}, bf16[32,13,128]{2,0,1:T(8,128)(2,1)S(1)}, u32[]{:S(2)}, u32[]{:S(2)}) collective-permute-start(bf16[32,13,128]{2,0,1:T(8,128)(2,1)S(1)} %get-tuple-element.15), channel_id=1, source_target_pairs={{0,504},{8,0},{16,8},{24,16},{32,24},{40,32},{48,40},{56,48},{64,5... | collective-permute-start | bytes 319496 | tf_op jit(solution)/shard_map/ppermute | solution.py:11
  187.6 2.4 copy.87
  190.1 3.7 %gather_fusion.5 = f32[256,32,13]{1,2,0:T(8,128)} fusion(f32[32,13,256]{0,1,2:T(8,128)} %copy.87, s32[1024]{0:T(1024)S(1)} %pad_clamp_fusion), kind=kCustom, calls=%fused_computation.3.clone | custom fusion | bytes 852992 | tf_op jit(solution)/shard_map/jit(_take)/gather | solution.py:16
  193.7 3.7 %gather_fusion.4 = f32[256,32,13]{1,2,0:T(8,128)} fusion(f32[32,13,256]{0,1,2:T(8,128)} %copy.87, s32[1024]{0:T(1024)S(1)} %pad_clamp_fusion.1), kind=kCustom, calls=%fused_computation.2.clone | custom fusion | bytes 852992 | tf_op jit(solution)/shard_map/jit(_take)/gather | solution.py:15
  197.4 4.4 %fusion = f32[256,32,13]{1,2,0:T(8,128)} fusion(bf16[13,13,256]{0,1,2:T(8,128)(2,1)S(1)} %copy-done.1, f32[256,32,13]{1,2,0:T(8,128)} %gather_fusion.5, pred[256]{0:T(512)(128)(4,1)S(1)} %compare_and_fusion.1), kind=kOutput, calls=%fused_computation.10 | convolution fusion | flops 16719872 | bytes 938752 | tf_op jit(solution)/shard_map/bae,vbe->vae/dot_general | solution.py:18
  201.8 2.9 fusion.2
  204.8 20.3 %scatter_fusion.2 = f32[32,13,256]{0,1,2:T(8,128)S(1)} fusion(f32[32,13,256]{0,1,2:T(8,128)S(1)} %broadcast.20, s32[256]{0:T(256)S(1)} %get-tuple-element.19, f32[256,32,13]{1,2,0:T(8,128)} %fusion.2), kind=kCustom, calls=%fused_computation.8 | custom fusion | flops 106496 | bytes 1278976 | tf_op jit(solution)/shard_map/scatter-add | solution.py:20
  225.1 20.2 %scatter_fusion.3 = f32[32,13,256]{0,1,2:T(8,128)S(1)} fusion(f32[32,13,256]{0,1,2:T(8,128)S(1)} %scatter_fusion.2, s32[256]{0:T(256)S(1)} %compare_select_fusion.2, f32[256,32,13]{1,2,0:T(8,128)} %fusion), kind=kCustom, calls=%fused_computation.9 | custom fusion | flops 106496 | bytes 1278976 | tf_op jit(solution)/shard_map/scatter-add | solution.py:21
  248.3 13.0 %collective-permute-done.4 = bf16[32,13,128]{2,0,1:T(8,128)(2,1)S(1)} collective-permute-done((bf16[32,13,128]{2,0,1:T(8,128)(2,1)S(1)}, bf16[32,13,128]{2,0,1:T(8,128)(2,1)S(1)}, u32[]{:S(2)}, u32[]{:S(2)}) %collective-permute-start.4) | collective-permute-done | bytes 106528 | tf_op jit(solution)/shard_map/ppermute | solution.py:11
  262.2 31.3 %reduce-scatter.5.cloned.1.call-done = f32[4,13,128]{2,1,0:T(8,128)} async-done(((f32[32,13,128]{2,1,0:T(8,128)}), f32[4,13,128]{2,1,0:T(8,128)}) %reduce-scatter.5.cloned.1.call-update) | async-done | bytes 26640 | tf_op jit(solution)/shard_map/reduce_scatter | solution.py:68
  (69 shorter events, 25.6 us)
Async XLA Ops:
  7.2 40.6 %copy-start = (bf16[256,256]{1,0:T(8,128)(2,1)S(1)}, bf16[256,256]{1,0:T(8,128)(2,1)}, u32[]{:S(2)}) copy-start(bf16[256,256]{1,0:T(8,128)(2,1)} %param.19) | copy-start | bytes 393220
  7.2 40.6 %copy-start.3 = (bf16[128,256]{1,0:T(8,128)(2,1)S(1)}, bf16[128,256]{1,0:T(8,128)(2,1)}, u32[]{:S(2)}) copy-start(bf16[128,256]{1,0:T(8,128)(2,1)} %param.13) | copy-start | bytes 196612
  7.2 151.0 %reduce-scatter.3.cloned.1.call-start = ((), (), s32[]{:S(2)}) async-start(), calls=%async_computation.2 | async-start | bytes 294912 | tf_op jit(solution)/shard_map/reduce_scatter | solution.py:68
  7.2 40.5 %collective-permute-start = (bf16[128,256]{1,0:T(8,128)(2,1)}, bf16[128,256]{1,0:T(8,128)(2,1)S(1)}, u32[]{:S(2)}, u32[]{:S(2)}) collective-permute-start(bf16[128,256]{1,0:T(8,128)(2,1)} %param.13), channel_id=1, source_target_pairs={{0,504},{8,0},{16,8},{24,16},{32,24},{40,32},{48,40},{56,48},{64,5... | collective-permute-start | bytes 196616 | tf_op jit(solution)/shard_map/ppermute | solution.py:11
  39.8 13.2 %collective-permute-start.1 = (bf16[32,13,128]{2,0,1:T(8,128)(2,1)S(1)}, bf16[32,13,128]{2,0,1:T(8,128)(2,1)S(1)}, u32[]{:S(2)}, u32[]{:S(2)}) collective-permute-start(bf16[32,13,128]{2,0,1:T(8,128)(2,1)S(1)} %get-tuple-element.17), channel_id=1, source_target_pairs={{0,504},{8,0},{16,8},{24,16},{32,24},{40,32},{48,40},{56,48},{64,5... | collective-permute-start | bytes 319496 | tf_op jit(solution)/shard_map/ppermute | solution.py:11
  46.8 2.2 copy-start.8
  46.8 2.2 copy-start.9
  47.8 1.5 copy-start.6
  48.0 1.5 copy-start.7
  49.9 3.1 %copy-start.5 = (bf16[169,256]{1,0:T(8,128)(2,1)}, bf16[169,256]{1,0:T(8,128)(2,1)S(1)}, u32[]{:S(2)}) copy-start(bf16[169,256]{1,0:T(8,128)(2,1)S(1)} %fusion.13) | copy-start | bytes 259588
  112.4 14.3 %collective-permute-start.2 = (bf16[32,13,128]{2,0,1:T(8,128)(2,1)S(1)}, bf16[32,13,128]{2,0,1:T(8,128)(2,1)S(1)}, u32[]{:S(2)}, u32[]{:S(2)}) collective-permute-start(bf16[32,13,128]{2,0,1:T(8,128)(2,1)S(1)} %copy.97), channel_id=1, source_target_pairs={{0,8},{8,16},{16,24},{24,32},{32,40},{40,48},{48,56},{56,64},{64,7... | collective-permute-start | bytes 319496 | tf_op jit(solution)/shard_map/ppermute | solution.py:11
  127.6 165.9 %reduce-scatter.5.cloned.1.call-start = ((), (), s32[]{:S(2)}) async-start(), calls=%async_computation.3 | async-start | bytes 294912 | tf_op jit(solution)/shard_map/reduce_scatter | solution.py:68
  175.8 11.7 %collective-permute-start.3 = (bf16[32,13,128]{2,0,1:T(8,128)(2,1)S(1)}, bf16[32,13,128]{2,0,1:T(8,128)(2,1)S(1)}, u32[]{:S(2)}, u32[]{:S(2)}) collective-permute-start(bf16[32,13,128]{2,0,1:T(8,128)(2,1)S(1)} %get-tuple-element.15), channel_id=1, source_target_pairs={{0,504},{8,0},{16,8},{24,16},{32,24},{40,32},{48,40},{56,48},{64,5... | collective-permute-start | bytes 319496 | tf_op jit(solution)/shard_map/ppermute | solution.py:11
  187.6 9.8 %copy-start.1 = (bf16[13,13,256]{0,1,2:T(8,128)(2,1)S(1)}, bf16[13,13,256]{0,1,2:T(8,128)(2,1)}, u32[]{:S(2)}) copy-start(bf16[13,13,256]{0,1,2:T(8,128)(2,1)} %copy.81) | copy-start | bytes 259588
  197.4 4.4 %copy-start.2 = (f32[256,32,13]{1,2,0:T(8,128)S(1)}, f32[256,32,13]{1,2,0:T(8,128)}, u32[]{:S(2)}) copy-start(f32[256,32,13]{1,2,0:T(8,128)} %gather_fusion.4) | copy-start | bytes 1277956
  245.8 47.7 %copy-start.4 = (f32[4,13,128]{2,0,1:T(4,128)S(1)}, f32[4,13,128]{2,0,1:T(4,128)}, u32[]{:S(2)}) copy-start(f32[4,13,128]{2,0,1:T(4,128)} %param.23) | copy-start | bytes 79876
  245.8 15.5 %collective-permute-start.4 = (bf16[32,13,128]{2,0,1:T(8,128)(2,1)S(1)}, bf16[32,13,128]{2,0,1:T(8,128)(2,1)S(1)}, u32[]{:S(2)}, u32[]{:S(2)}) collective-permute-start(bf16[32,13,128]{2,0,1:T(8,128)(2,1)S(1)} %copy.99), channel_id=1, source_target_pairs={{0,8},{8,16},{16,24},{24,32},{32,40},{40,48},{48,56},{56,64},{64,7... | collective-permute-start | bytes 319496 | tf_op jit(solution)/shard_map/ppermute | solution.py:11
Sparse Core Ops, SparseCore 0:
  127.7 30.4 reduce-scatter.2
  262.4 31.1 reduce-scatter.4
where the time goes:
time: 306 us; the launch traced here: 302 us
  other arithmetic  86.2 us (28%)
  waiting for transfers between devices  85.8 us (28%)
  starting transfers between devices  33.8 us (11%)
  blocking collectives  32.6 us (11%)
  local copies, waits for them, and re-layouts  30.8 us (10%)
  matrix products  18.1 us (6%)
  between operations  14.4 us (5%)
    reduce_scatter x2, waiting for transfers between devices, operator(): return lax.psum_scatter(summed, 'vec', scatter_dimension=0, tiled=True)  61.8 us
    scatter-add x2, other arithmetic, apply_pairs(): result = result.at[:, :, sources].add(to_first)  40.5 us
    scatter-add x2, other arithmetic, apply_pairs(): return result.at[:, :, targets].add(to_second)  40.5 us
    ppermute x5, starting transfers between devices, shifted(): lax.ppermute(x, axis, [(i, (i + by) % length) for i in range(length)])  33.8 us
    all_gather x2, blocking collectives, operator(): every = lax.all_gather(vectors, 'vec', axis=0, tiled=True)  32.6 us
    ppermute x5, waiting for transfers between devices, shifted(): lax.ppermute(x, axis, [(i, (i + by) % length) for i in range(length)])  24 us
    dot_general x2, matrix products, apply_pairs(): jnp.einsum('bae,vbe->vae', blocks, at_sources, precision=lax.Precision.HI...  8.86 us
    dot_general x2, matrix products, apply_pairs(): jnp.einsum('abe,vbe->vae', blocks, at_targets, precision=lax.Precision.HI...  7.08 us
  transfers between devices with their start and end apart: 7, of which 5 were waited for; matrix products, arithmetic and copies ran while one was open for 5% of the time, Pallas kernels for 0%

commit v1 on v0

v1 whole, which is shorter than its diff:
```python
import math

import jax
import jax.numpy as jnp
from jax import lax
from jax.experimental import pallas as pl
from jax.experimental.pallas import tpu as pltpu
from jax.sharding import PartitionSpec as P

F32, BF16 = jnp.float32, jnp.bfloat16
MESH = pl.DeviceIdType.MESH
CHIPS = 4
SLOTS = [(k, r) for k in range(CHIPS) for r in range(2)]
PEERS = SLOTS[1:]
PAD = 16


def silu(v):
    half = 0.5 * v
    return half + half * jnp.tanh(half)


def mm(a, b):
    return jnp.dot(a, b, preferred_element_type=F32)


def mm_nt(a, b):
    return lax.dot_general(a, b, (((1,), (1,)), ((), ())), preferred_element_type=F32)


def transposed(x):
    return x.astype(F32).T.astype(BF16)


def kernel(
    feat_hbm, radial_hbm, src_ref, dst_ref, live_ref, ws_hbm, wd_hbm, wr_hbm, wh_hbm, wo_hbm, sv_hbm,
    blocks_hbm, out_ref,
    feat, ghost, rad, ws, wd, wr, wh, wo, sv,
    info, onehot, ha, hb, xs, xt, ys, yt,
    v_own, v_gh, proj, wht, wrt, wa, pb, blocks,
    gh_out, own_out, gh_in, own_in, gh2_out, gh2_in,
    local_sem, send_sem, recv_sem,
):
    n_space = lax.axis_size("space")
    d = lax.axis_index("space")
    j = lax.axis_index("vec")
    z, c = j // 2, j % 2
    zk = [z, z + 1 - 2 * (z % 2), (z + 2) % 4, 3 - z]
    left = (lax.rem(d + n_space - 1, n_space), j)
    right = (lax.rem(d + 1, n_space), j)
    at = [[(d, zk[k] * 2 + (c if r == 0 else 1 - c)) for r in range(2)] for k in range(CHIPS)]
    orb = out_ref.shape[1]
    nv = out_ref.shape[0]

    barrier = pltpu.get_barrier_semaphore()
    for dev in [left, right] + [at[k][r] for k, r in PEERS]:
        pl.semaphore_signal(barrier, inc=1, device_id=dev, device_id_type=MESH)

    loads = []
    for i, (a, b) in enumerate(
        [(sv_hbm, sv), (feat_hbm, feat), (ws_hbm, ws), (wd_hbm, wd), (wr_hbm, wr), (wh_hbm, wh), (wo_hbm, wo), (radial_hbm, rad.at[0])]
    ):
        cp = pltpu.make_async_copy(a, b, local_sem.at[i])
        cp.start()
        loads.append(cp)

    for row, ref in enumerate((src_ref, dst_ref, live_ref)):
        for h in range(2):
            info[0, 2 * row + h : 2 * row + h + 1, :] = ref[h * 128 : (h + 1) * 128].reshape(1, 128)
    info[0, 6:8, :] = jnp.zeros((2, 128), jnp.int32)
    loads[0].wait()
    v_own[...] = jnp.zeros_like(v_own)
    start = jnp.concatenate(
        [jnp.concatenate([sv[v], jnp.zeros((PAD - orb, 128), F32)], 0) for v in range(nv)], 0
    )
    v_own[0] = start.astype(BF16)

    pl.semaphore_wait(barrier, 2 + len(PEERS))

    sent = []

    def send(i, a, b, dev):
        cp = pltpu.make_async_remote_copy(
            src_ref=a, dst_ref=b, send_sem=send_sem.at[i], recv_sem=recv_sem.at[i],
            device_id=dev, device_id_type=MESH,
        )
        cp.start()
        sent.append(cp)
        return cp

    mine = pl.ds(pl.multiple_of(j * 16, 16), 16)
    piece_in = send(0, feat_hbm.at[mine, :], ghost.at[mine, :], left)
    info_in = {}
    for n, (k, r) in enumerate(PEERS):
        s = 2 * k + r
        info_in[s] = send(5 + n, info.at[0], info.at[s], at[k][r])
    rad_in = {}
    for k in (1, 3, 2):
        rad_in[k] = send(1 + k, radial_hbm, rad.at[k], at[k][0])
    vgh_in = send(1, v_own.at[0], v_gh.at[0], left)

    def make_onehot(s):
        rows = lax.broadcasted_iota(jnp.int32, (256, 128), 0)
        for h in range(2):
            lanes = slice(h * 128, (h + 1) * 128)
            onehot[s, 0:128, lanes] = jnp.where(rows[:128] == info[s, h : h + 1, :], 1.0, 0.0).astype(BF16)
            onehot[s, 128:384, lanes] = jnp.where(rows == info[s, 2 + h : 3 + h, :], 1.0, 0.0).astype(BF16)

    make_onehot(0)
    for cp in loads[1:]:
        cp.wait()

    piece_in.wait_recv()
    ghost_in = []
    for n, (k, r) in enumerate(PEERS):
        ghost_in.append(send(12 + n, ghost.at[mine, :], ghost.at[mine, :], at[k][r]))

    for layer in range(wh.shape[0]):
        wht[layer] = transposed(wh[layer])
    wrt[...] = transposed(wr[...])
    rows = lax.broadcasted_iota(jnp.int32, (13 * PAD, 169), 0)
    cols = lax.broadcasted_iota(jnp.int32, (13 * PAD, 169), 1)
    outer, inner = lax.shift_right_logical(rows, 4), lax.bitwise_and(rows, 15)
    spread = jnp.where((inner < orb) & (cols == outer * orb + inner), 1.0, 0.0).astype(BF16)
    wa[...] = mm(spread, wo[...]).astype(BF16)
    rows = lax.broadcasted_iota(jnp.int32, (13 * PAD, 13 * PAD), 0)
    cols = lax.broadcasted_iota(jnp.int32, (13 * PAD, 13 * PAD), 1)
    outer, inner = lax.shift_right_logical(rows, 4), lax.bitwise_and(rows, 15)
    pb[...] = jnp.where((inner < orb) & (cols == inner * PAD + outer), 1.0, 0.0).astype(BF16)
    proj[:, 0:128] = transposed(mm(feat[...], ws[...]))
    proj[:, 128:256] = transposed(mm(feat[...], wd[...]))

    for k, r in PEERS:
        s = 2 * k + r
        info_in[s].wait_recv()
        make_onehot(s)

    for cp in ghost_in:
        cp.wait_recv()
    proj[:, 256:384] = transposed(mm(ghost[...], wd[...]))

    def live_row(s):
        return jnp.concatenate([info[s, 4:5, :], info[s, 5:6, :]], 1).astype(F32)

    def network(k):
        s = 2 * k
        pre = mm(proj[...], onehot[s]) + mm_nt(wrt[...], rad[k])
        hidden = silu(pre).astype(BF16)
        for layer in range(wh.shape[0]):
            hidden = (hidden.astype(F32) + silu(mm(wht[layer], hidden))).astype(BF16)
        live = live_row(s)
        ha[s] = (mm(wa[...], hidden) * live).astype(BF16)
        if k == 0:
            blocks[...] = (mm(wo[...], hidden) * live).astype(BF16)

    def to_targets(s, vec):
        xs[...] = mm(vec, onehot[s, 0:128, :]).reshape(nv, PAD, 256)
        acc = jnp.zeros((nv, PAD, 256), F32)
        for a in range(orb):
            acc += ha[s, a * PAD : (a + 1) * PAD, :].astype(F32)[None] * xs[:, a : a + 1, :]
        return acc.reshape(nv * PAD, 256).astype(BF16)

    def to_sources(s, vec):
        xt[...] = mm(vec, onehot[s, 128:384, :]).reshape(nv, PAD, 256)
        acc = jnp.zeros((nv, PAD, 256), F32)
        for b in range(orb):
            acc += hb[s, b * PAD : (b + 1) * PAD, :][None] * xt[:, b : b + 1, :]
        return acc.reshape(nv * PAD, 256).astype(BF16)

    def at_targets(s, y):
        return mm_nt(y, onehot[s, 128:384, :])

    def at_sources(s, y):
        return mm_nt(y, onehot[s, 0:128, :])

    h_in = []
    p_t = jnp.zeros((nv * PAD, 256), F32)
    p_s = jnp.zeros((nv * PAD, 128), F32)

    def first_apply(s):
        hb[s] = mm(pb[...], ha[s])
        own = v_own[0]
        both = jnp.concatenate([own, v_gh[0]], 1)
        return at_targets(s, to_targets(s, own)), at_sources(s, to_sources(s, both))

    for k in range(CHIPS):
        if k:
            rad_in[k].wait_recv()
        network(k)
        h_in.append(send(19 + k, ha.at[2 * k], ha.at[2 * k + 1], at[0][1]))
        if k == 0:
            blocks_out = pltpu.make_async_copy(blocks, blocks_hbm, local_sem.at[8])
            blocks_out.start()
            vgh_in.wait_recv()
        dt, ds = first_apply(2 * k)
        p_t, p_s = p_t + dt, p_s + ds
        h_in[k].wait_recv()
        dt, ds = first_apply(2 * k + 1)
        p_t, p_s = p_t + dt, p_s + ds

    part_gh = p_t[:, 128:]
    part_own = p_s + p_t[:, :128]
    gh_out[...] = part_gh.astype(BF16)
    gh_in_cp = send(23, gh_out, gh_in, right)
    own_out[...] = part_own.astype(BF16)
    own_in_cp = send(24, own_out, own_in, left)
    gh_in_cp.wait_recv()
    own1 = (part_own + gh_in[...].astype(F32)).astype(BF16)

    p_t = jnp.zeros((nv * PAD, 256), F32)
    for s in range(2 * CHIPS):
        p_t += at_targets(s, to_targets(s, own1))
    gh2_out[...] = p_t[:, 128:].astype(BF16)
    gh2_in_cp = send(25, gh2_out, gh2_in, right)
    own_in_cp.wait_recv()
    gh1 = (part_gh + own_in[...].astype(F32)).astype(BF16)
    both1 = jnp.concatenate([own1, gh1], 1)
    p_s = jnp.zeros((nv * PAD, 128), F32)
    for s in range(2 * CHIPS):
        p_s += at_sources(s, to_sources(s, both1))
    gh2_in_cp.wait_recv()
    second = p_s + p_t[:, :128] + gh2_in[...].astype(F32)
    for v in range(nv):
        out_ref[v] = 2.0 * second[v * PAD : v * PAD + orb] - sv[v]
    blocks_out.wait()
    for cp in sent:
        cp.wait_send()


def on_device(node_feat, radial, edge_src, edge_dst, edge_live, w_src, w_dst, w_radial, w_hidden, w_out, start_vectors):
    anywhere = pl.BlockSpec(memory_space=pl.ANY)
    vmem = pl.BlockSpec(memory_space=pltpu.VMEM)
    edges = radial.shape[0]
    nv, orb, atoms = start_vectors.shape
    width = node_feat.shape[1]
    rows = 13 * PAD
    vec = nv * PAD

    def scratch(*shape, dtype=BF16):
        return pltpu.VMEM(shape, dtype)

    return pl.pallas_call(
        kernel,
        out_shape=(
            jax.ShapeDtypeStruct((w_out.shape[0], edges), BF16),
            jax.ShapeDtypeStruct(start_vectors.shape, F32),
        ),
        in_specs=[anywhere, anywhere, vmem, vmem, vmem] + [anywhere] * 6,
        out_specs=(anywhere, vmem),
        scratch_shapes=[
            scratch(atoms, width),
            scratch(atoms, width),
            scratch(CHIPS, edges, radial.shape[1]),
            scratch(*w_src.shape),
            scratch(*w_dst.shape),
            scratch(*w_radial.shape),
            scratch(*w_hidden.shape),
            scratch(*w_out.shape),
            scratch(*start_vectors.shape, dtype=F32),
            scratch(8, 8, 128, dtype=jnp.int32),
            scratch(8, 3 * atoms, edges),
            scratch(8, rows, edges),
            scratch(8, rows, edges, dtype=F32),
            scratch(nv, PAD, edges, dtype=F32),
            scratch(nv, PAD, edges, dtype=F32),
            scratch(8, vec, edges),
            scratch(8, vec, edges),
            scratch(1, vec, atoms),
            scratch(1, vec, atoms),
            scratch(width, 3 * atoms),
            scratch(*w_hidden.shape),
            scratch(width, radial.shape[1]),
            scratch(rows, width),
            scratch(rows, rows),
            scratch(w_out.shape[0], edges),
        ]
        + [scratch(vec, atoms)] * 6
        + [
            pltpu.SemaphoreType.DMA((9,)),
            pltpu.SemaphoreType.DMA((26,)),
            pltpu.SemaphoreType.DMA((26,)),
        ],
        compiler_params=pltpu.CompilerParams(
            collective_id=0, has_side_effects=True, vmem_limit_bytes=40 * 1024 * 1024
        ),
        name="pair_filter",
    )(node_feat, radial, edge_src, edge_dst, edge_live, w_src, w_dst, w_radial, w_hidden, w_out, start_vectors)


def solution(mesh):
    in_specs = (
        P("space", None),
        P(("space", "vec"), None),
        P(("space", "vec")),
        P(("space", "vec")),
        P(("space", "vec")),
        P(),
        P(),
        P(),
        P(),
        P(),
        P("vec", None, "space"),
    )
    out_specs = (P(None, ("space", "vec")), P("vec", None, "space"))
    return jax.shard_map(
        on_device, mesh=mesh, in_specs=in_specs, out_specs=out_specs, check_vma=False
    )
```

time: 306 us -> 56 us (0.18); the launches traced: 302 us -> 55 us
  other arithmetic: 86.2 us -> 0 us
  waiting for transfers between devices: 85.8 us -> 0 us
  Pallas kernels: 0 us -> 46.1 us
  starting transfers between devices: 33.8 us -> 0 us
  blocking collectives: 32.6 us -> 0 us
  local copies, waits for them, and re-layouts: 30.8 us -> 8.19 us
  matrix products: 18.1 us -> 0 us
  between operations: 14.4 us -> 0.69 us
    scatter-add x4 -> x0, other arithmetic: 81 us -> none  [the longest x2 40.5 us: apply_pairs(): result = result.at[:, :, sources].add(to_first)]
    reduce_scatter x2 -> x0, waiting for transfers between devices: 61.8 us -> none  [operator(): return lax.psum_scatter(summed, 'vec', scatter_dimension=0, tiled=True)]
    pallas_call x0 -> x1, Pallas kernels: none -> 46.1 us  [on_device(): pl.pallas_call(kernel, out_shape=(jax.ShapeDtypeStruct((w_out.shape[0], e...]
    ppermute x5 -> x0, starting transfers between devices: 33.8 us -> none  [shifted(): lax.ppermute(x, axis, [(i, (i + by) % length) for i in range(length)])]
    all_gather x2 -> x0, blocking collectives: 32.6 us -> none  [operator(): every = lax.all_gather(vectors, 'vec', axis=0, tiled=True)]
    ppermute x5 -> x0, waiting for transfers between devices: 24 us -> none  [shifted(): lax.ppermute(x, axis, [(i, (i + by) % length) for i in range(length)])]
    dot_general x9 -> x0, matrix products: 18.1 us -> none  [the longest x2 8.86 us: apply_pairs(): jnp.einsum('bae,vbe->vae', blocks, at_sources, precision=lax.Precision.HI...]
    gather x6 -> x0, local copies, waits for them, and re-layouts: 14 us -> none  [the longest x2 6.02 us: apply_pairs(): at_targets = jnp.take(vectors, targets, axis=2)]
  transfers between devices with their start and end apart: 7 -> 0, of which waited for: 5 -> 0; matrix products, arithmetic and copies ran while one was open for 5% -> 0% of each run, Pallas kernels for 0% -> 0%
where the time goes in v1:
time: 56 us; the launch traced here: 55 us
  Pallas kernels  46.1 us (82%)
  local copies, waits for them, and re-layouts  8.19 us (15%)
  between operations  0.69 us (1%)
    pallas_call x1, Pallas kernels, on_device(): pl.pallas_call(kernel, out_shape=(jax.ShapeDtypeStruct((w_out.shape[0], e...  46.1 us
    unnamed x22, local copies, waits for them, and re-layouts  7.57 us

profile of v1, /device:TPU:1, one launch (start us, length us, event | category | flops | bytes accessed | tf_op | source)
XLA Modules:
  0.0 55.0 jit_solution(13577016042031876131)
XLA Ops:
  0.6 0.0 copy-start.9
  0.6 0.0 copy-start.8
  0.7 0.0 copy-start.7
  0.7 0.8 %copy.13.sv_hbm = f32[4,13,128]{2,1,0:T(8,128)S(1)} copy(f32[4,13,128]{2,0,1:T(4,128)} %param.21) | data formatting | bytes 53248 | tf_op args[10]
  1.4 0.0 copy-done.9
  1.4 0.0 copy-done.8
  1.4 0.0 copy-done.7
  1.4 0.0 copy-start
  1.5 0.9 %copy-done = bf16[2,256,256]{2,1,0:T(8,128)(2,1)S(1)} copy-done((bf16[2,256,256]{2,1,0:T(8,128)(2,1)S(1)}, bf16[2,256,256]{2,1,0:T(8,128)(2,1)}, u32[]{:S(2)}) %copy-start) | copy-done | bytes 262168
  2.4 0.0 copy-start.1
  2.4 0.9 %copy-done.1 = bf16[256,256]{1,0:T(8,128)(2,1)S(1)} copy-done((bf16[256,256]{1,0:T(8,128)(2,1)S(1)}, bf16[256,256]{1,0:T(8,128)(2,1)}, u32[]{:S(2)}) %copy-start.1) | copy-done | bytes 131096
  3.3 0.0 copy-start.2
  3.3 0.9 %copy-done.2 = bf16[256,256]{1,0:T(8,128)(2,1)S(1)} copy-done((bf16[256,256]{1,0:T(8,128)(2,1)S(1)}, bf16[256,256]{1,0:T(8,128)(2,1)}, u32[]{:S(2)}) %copy-start.2) | copy-done | bytes 131096
  4.2 0.0 copy-start.3
  4.2 0.9 %copy-done.3 = bf16[169,256]{1,0:T(8,128)(2,1)S(1)} copy-done((bf16[169,256]{1,0:T(8,128)(2,1)S(1)}, bf16[169,256]{1,0:T(8,128)(2,1)}, u32[]{:S(2)}) %copy-start.3) | copy-done | bytes 86552
  5.1 0.0 copy-start.4
  5.1 0.8 %copy-done.4 = bf16[128,256]{1,0:T(8,128)(2,1)S(1)} copy-done((bf16[128,256]{1,0:T(8,128)(2,1)S(1)}, bf16[128,256]{1,0:T(8,128)(2,1)}, u32[]{:S(2)}) %copy-start.4) | copy-done | bytes 65560
  5.9 0.0 copy-start.5
  5.9 0.8 %copy-done.5 = bf16[256,128]{1,0:T(8,128)(2,1)S(1)} copy-done((bf16[256,128]{1,0:T(8,128)(2,1)S(1)}, bf16[256,128]{1,0:T(8,128)(2,1)}, u32[]{:S(2)}) %copy-start.5) | copy-done | bytes 65560
  6.8 0.0 copy-start.6
  6.8 0.8 %copy-done.6 = bf16[128,256]{1,0:T(8,128)(2,1)S(1)} copy-done((bf16[128,256]{1,0:T(8,128)(2,1)S(1)}, bf16[128,256]{1,0:T(8,128)(2,1)}, u32[]{:S(2)}) %copy-start.6) | copy-done | bytes 65560
  7.6 46.1 %pair_filter.1 = (bf16[169,256]{1,0:T(8,128)(2,1)S(1)}, f32[4,13,128]{2,1,0:T(8,128)S(1)}) custom-call(bf16[128,256]{1,0:T(8,128)(2,1)S(1)} %copy-done.4, bf16[256,128]{1,0:T(8,128)(2,1)S(1)} %copy-done.5, s32[256]{0:T(256)S(1)} %copy-done.7, s32[256]{0:T(256)S(1)} %copy-done.8, s32[256]{0:T(256)S(1)} %copy-done.9, bf16[256,256]{1,0:T(8,128)(2,1)S(1)} %copy-done.1, ...), custom_call_target="tpu_custom_call" | custom-call | tf_op jit(solution)/shard_map/pair_filter/pallas_call | solution.py:242
  53.7 0.6 %copy.14 = f32[4,13,128]{2,0,1:T(4,128)} copy(f32[4,13,128]{2,1,0:T(8,128)S(1)} %get-tuple-element.3) | data formatting | bytes 53248 | tf_op jit(solution)/shard_map/pair_filter/pallas_call | solution.py:242
  54.4 0.6 %copy.16 = bf16[169,256]{1,0:T(8,128)(2,1)} copy(bf16[169,256]{1,0:T(8,128)(2,1)S(1)} %get-tuple-element.6) | data formatting | bytes 173056
Async XLA Ops:
  0.6 0.8 %copy-start.9 = (s32[256]{0:T(256)S(1)}, s32[256]{0:T(256)}, u32[]{:S(2)}) copy-start(s32[256]{0:T(256)} %live_ref.1) | copy-start | bytes 3076
  0.6 0.8 %copy-start.8 = (s32[256]{0:T(256)S(1)}, s32[256]{0:T(256)}, u32[]{:S(2)}) copy-start(s32[256]{0:T(256)} %dst_ref.1) | copy-start | bytes 3076
  0.7 0.8 %copy-start.7 = (s32[256]{0:T(256)S(1)}, s32[256]{0:T(256)}, u32[]{:S(2)}) copy-start(s32[256]{0:T(256)} %src_ref.1) | copy-start | bytes 3076
  1.4 1.0 %copy-start = (bf16[2,256,256]{2,1,0:T(8,128)(2,1)S(1)}, bf16[2,256,256]{2,1,0:T(8,128)(2,1)}, u32[]{:S(2)}) copy-start(bf16[2,256,256]{2,1,0:T(8,128)(2,1)} %wh_hbm.1) | copy-start | bytes 786436
  2.4 0.9 %copy-start.1 = (bf16[256,256]{1,0:T(8,128)(2,1)S(1)}, bf16[256,256]{1,0:T(8,128)(2,1)}, u32[]{:S(2)}) copy-start(bf16[256,256]{1,0:T(8,128)(2,1)} %ws_hbm.1) | copy-start | bytes 393220
  3.3 0.9 %copy-start.2 = (bf16[256,256]{1,0:T(8,128)(2,1)S(1)}, bf16[256,256]{1,0:T(8,128)(2,1)}, u32[]{:S(2)}) copy-start(bf16[256,256]{1,0:T(8,128)(2,1)} %wd_hbm.1) | copy-start | bytes 393220
  4.2 0.9 %copy-start.3 = (bf16[169,256]{1,0:T(8,128)(2,1)S(1)}, bf16[169,256]{1,0:T(8,128)(2,1)}, u32[]{:S(2)}) copy-start(bf16[169,256]{1,0:T(8,128)(2,1)} %wo_hbm.1) | copy-start | bytes 259588
  5.1 0.8 %copy-start.4 = (bf16[128,256]{1,0:T(8,128)(2,1)S(1)}, bf16[128,256]{1,0:T(8,128)(2,1)}, u32[]{:S(2)}) copy-start(bf16[128,256]{1,0:T(8,128)(2,1)} %feat_hbm.1) | copy-start | bytes 196612
  5.9 0.8 %copy-start.5 = (bf16[256,128]{1,0:T(8,128)(2,1)S(1)}, bf16[256,128]{1,0:T(8,128)(2,1)}, u32[]{:S(2)}) copy-start(bf16[256,128]{1,0:T(8,128)(2,1)} %radial_hbm.1) | copy-start | bytes 196612
  6.8 0.8 %copy-start.6 = (bf16[128,256]{1,0:T(8,128)(2,1)S(1)}, bf16[128,256]{1,0:T(8,128)(2,1)}, u32[]{:S(2)}) copy-start(bf16[128,256]{1,0:T(8,128)(2,1)} %wr_hbm.1) | copy-start | bytes 196612

commit v2 on v1

v2 whole, which is shorter than its diff:
```python
import math

import jax
import jax.numpy as jnp
from jax import lax
from jax.experimental import pallas as pl
from jax.experimental.pallas import tpu as pltpu
from jax.sharding import PartitionSpec as P

F32, BF16 = jnp.float32, jnp.bfloat16
MESH = pl.DeviceIdType.MESH
CHIPS = 4
PAD = 16


def silu(v):
    half = 0.5 * v
    return half + half * jnp.tanh(half)


def mm(a, b):
    return jnp.dot(a, b, preferred_element_type=F32)


def mm_nt(a, b):
    return lax.dot_general(a, b, (((1,), (1,)), ((), ())), preferred_element_type=F32)


def transposed(x):
    return x.astype(F32).T.astype(BF16)


def kernel(
    feat_hbm, radial_hbm, src_ref, dst_ref, live_ref, ws_hbm, wd_hbm, wr_hbm, wh_hbm, wo_hbm, sv_hbm,
    blocks_hbm, out_ref,
    feat, ghost, rad, ws, wd, wr, wh, wo, sv,
    info, onehot, ha, hb, xs, xt, pre,
    v_own, v_gh, proj, wht, wrt, wdt, wa, pb, blocks,
    gh_out, own_out, gh_in, own_in, gh2_out, gh2_in,
    local_sem, send_sem, recv_sem,
):
    n_space = lax.axis_size("space")
    d = lax.axis_index("space")
    j = lax.axis_index("vec")
    z, c = j // 2, j % 2
    zk = [z, z + 1 - 2 * (z % 2), (z + 2) % 4, 3 - z]
    left = (lax.rem(d + n_space - 1, n_space), j)
    right = (lax.rem(d + 1, n_space), j)
    same = [(d, zk[k] * 2 + c) for k in range(CHIPS)]
    sibling = (d, z * 2 + 1 - c)
    orb, nv = out_ref.shape[:2]
    layers = wh.shape[0]

    partners = [left, right, sibling] + same[1:]
    barrier = pltpu.get_barrier_semaphore()
    for dev in partners:
        pl.semaphore_signal(barrier, inc=1, device_id=dev, device_id_type=MESH)

    loads = []
    for i, (a, b) in enumerate(
        [(sv_hbm, sv), (feat_hbm, feat), (ws_hbm, ws), (wd_hbm, wd), (wr_hbm, wr), (wh_hbm, wh), (wo_hbm, wo), (radial_hbm, rad.at[0])]
    ):
        cp = pltpu.make_async_copy(a, b, local_sem.at[i])
        cp.start()
        loads.append(cp)

    for row, ref in enumerate((src_ref, dst_ref, live_ref)):
        for h in range(2):
            info[0, 2 * row + h : 2 * row + h + 1, :] = ref[h * 128 : (h + 1) * 128].reshape(1, 128)
    info[0, 6:8, :] = jnp.zeros((2, 128), jnp.int32)
    loads[0].wait()
    start = jnp.concatenate(
        [jnp.concatenate([sv[:, v, :], jnp.zeros((PAD - orb, 128), F32)], 0) for v in range(nv)], 0
    )
    v_own[...] = start.astype(BF16)

    pl.semaphore_wait(barrier, len(partners))

    sent = []

    def send(i, a, b, dev):
        cp = pltpu.make_async_remote_copy(
            src_ref=a, dst_ref=b, send_sem=send_sem.at[i], recv_sem=recv_sem.at[i],
            device_id=dev, device_id_type=MESH,
        )
        cp.start()
        sent.append(cp)
        return cp

    half = pl.ds(pl.multiple_of(c * 64, 64), 64)
    half_in = send(0, feat_hbm.at[half, :], ghost.at[half, :], left)
    vgh_in = send(1, v_own, v_gh, left)
    info_in = [send(1 + k, info.at[0], info.at[k], same[k]) for k in (1, 2, 3)]
    rad_in = [send(4 + k, radial_hbm, rad.at[k], same[k]) for k in (1, 3, 2)]

    def make_onehot(k, r):
        s, t = 2 * k + r, 4 * r + k
        rows = lax.broadcasted_iota(jnp.int32, (256, 128), 0)
        for h in range(2):
            lanes = slice(h * 128, (h + 1) * 128)
            onehot[s, 0:128, lanes] = jnp.where(rows[:128] == info[t, h : h + 1, :], 1.0, 0.0).astype(BF16)
            to = jnp.where(rows == info[t, 2 + h : 3 + h, :], 1.0, 0.0).astype(BF16)
            onehot[s, 128:384, lanes] = to
            if r == 0:
                onehot[s, 384:512, lanes] = to[128:]

    make_onehot(0, 0)
    for cp in info_in:
        cp.wait_recv()
    info_sib = send(8, info.at[0:4], info.at[4:8], sibling)
    for cp in loads[1:]:
        cp.wait()

    wdt[...] = transposed(wd[...])
    for layer in range(layers):
        wht[layer] = transposed(wh[layer])
    wrt[...] = transposed(wr[...])
    rows = lax.broadcasted_iota(jnp.int32, (13 * PAD, 169), 0)
    cols = lax.broadcasted_iota(jnp.int32, (13 * PAD, 169), 1)
    outer, inner = lax.shift_right_logical(rows, 4), lax.bitwise_and(rows, 15)
    spread = jnp.where((inner < orb) & (cols == outer * orb + inner), 1.0, 0.0).astype(BF16)
    wa[...] = mm(spread, wo[...]).astype(BF16)
    rows = lax.broadcasted_iota(jnp.int32, (13 * PAD, 13 * PAD), 0)
    cols = lax.broadcasted_iota(jnp.int32, (13 * PAD, 13 * PAD), 1)
    outer, inner = lax.shift_right_logical(rows, 4), lax.bitwise_and(rows, 15)
    pb[...] = jnp.where((inner < orb) & (cols == inner * PAD + outer), 1.0, 0.0).astype(BF16)

    def halves(x):
        top = x.astype(BF16)
        return top, (x - top.astype(F32)).astype(BF16)

    for n, w in enumerate((transposed(ws[...]), wdt[...])):
        proj[0, :, n * 128 : (n + 1) * 128], proj[1, :, n * 128 : (n + 1) * 128] = halves(mm_nt(w, feat[...]))

    for k in range(1, CHIPS):
        make_onehot(k, 0)

    half_in.wait_recv()
    other_in = send(9, ghost.at[half, :], ghost.at[half, :], sibling)

    for cp in rad_in:
        cp.wait_recv()
    for k in range(CHIPS):
        pre[k] = (
            mm(proj[0], onehot[2 * k, 0:256, :]) + mm(proj[1], onehot[2 * k, 0:256, :]) + mm_nt(wrt[...], rad[k])
        )
    info_sib.wait_recv()
    for k in range(CHIPS):
        make_onehot(k, 1)

    other_in.wait_recv()
    proj[2, :, 0:128], proj[2, :, 128:256] = halves(mm_nt(wdt[...], ghost[...]))

    every = range(CHIPS)
    hidden = [silu(pre[k] + mm(proj[2], onehot[2 * k, 256:512, :])).astype(BF16) for k in every]
    for layer in range(layers):
        hidden = [(hidden[k].astype(F32) + silu(mm(wht[layer], hidden[k]))).astype(BF16) for k in every]
    h_in = []
    for k in every:
        live = jnp.concatenate([info[k, 4:5, :], info[k, 5:6, :]], 1).astype(F32)
        ha[2 * k] = (mm(wa[...], hidden[k]) * live).astype(BF16)
        h_in.append(send(10 + k, ha.at[2 * k], ha.at[2 * k + 1], sibling))
        if k == 0:
            blocks[...] = (mm(wo[...], hidden[0]) * live).astype(BF16)
    blocks_out = pltpu.make_async_copy(blocks, blocks_hbm, local_sem.at[8])
    blocks_out.start()

    def to_targets(s, vec):
        xs[s] = mm(vec, onehot[s, 0:128, :]).reshape(nv, PAD, 256)
        acc = jnp.zeros((nv, PAD, 256), F32)
        for a in range(orb):
            acc += ha[s, a * PAD : (a + 1) * PAD, :].astype(F32)[None] * xs[s, :, a : a + 1, :]
        return mm_nt(acc.reshape(nv * PAD, 256).astype(BF16), onehot[s, 128:384, :])

    def to_sources(s, vec):
        xt[s] = mm(vec, onehot[s, 128:384, :]).reshape(nv, PAD, 256)
        acc = jnp.zeros((nv, PAD, 256), F32)
        for b in range(orb):
            acc += hb[s, b * PAD : (b + 1) * PAD, :][None] * xt[s, :, b : b + 1, :]
        return mm_nt(acc.reshape(nv * PAD, 256).astype(BF16), onehot[s, 0:128, :])

    vgh_in.wait_recv()
    own = v_own[...]
    both = jnp.concatenate([own, v_gh[...]], 1)
    p_t = jnp.zeros((nv * PAD, 256), F32)
    p_s = jnp.zeros((nv * PAD, 128), F32)
    for s in range(0, 2 * CHIPS, 2):
        hb[s] = mm(pb[...], ha[s])
        p_t += to_targets(s, own)
        p_s += to_sources(s, both)
    for cp in h_in:
        cp.wait_recv()
    for s in range(1, 2 * CHIPS, 2):
        p_t += to_targets(s, own)
    part_gh = p_t[:, 128:]
    gh_out[...] = part_gh.astype(BF16)
    gh_in_cp = send(14, gh_out, gh_in, right)
    for s in range(1, 2 * CHIPS, 2):
        hb[s] = mm(pb[...], ha[s])
        p_s += to_sources(s, both)
    part_own = p_s + p_t[:, :128]
    own_out[...] = part_own.astype(BF16)
    own_in_cp = send(15, own_out, own_in, left)

    gh_in_cp.wait_recv()
    own1 = (part_own + gh_in[...].astype(F32)).astype(BF16)
    p_t = jnp.zeros((nv * PAD, 256), F32)
    for s in range(2 * CHIPS):
        p_t += to_targets(s, own1)
    gh2_out[...] = p_t[:, 128:].astype(BF16)
    gh2_in_cp = send(16, gh2_out, gh2_in, right)
    own_in_cp.wait_recv()
    gh1 = (part_gh + own_in[...].astype(F32)).astype(BF16)
    both1 = jnp.concatenate([own1, gh1], 1)
    p_s = jnp.zeros((nv * PAD, 128), F32)
    for s in range(2 * CHIPS):
        p_s += to_sources(s, both1)
    second = 2.0 * (p_s + p_t[:, :128])
    blocks_out.wait()
    for cp in sent:
        cp.wait_send()
    gh2_in_cp.wait_recv()
    second = second + 2.0 * gh2_in[...].astype(F32)
    for v in range(nv):
        out_ref[:, v, :] = second[v * PAD : v * PAD + orb] - sv[:, v, :]


def on_device(node_feat, radial, edge_src, edge_dst, edge_live, w_src, w_dst, w_radial, w_hidden, w_out, start_vectors):
    anywhere = pl.BlockSpec(memory_space=pltpu.HBM)
    vmem = pl.BlockSpec(memory_space=pltpu.VMEM)
    edges = radial.shape[0]
    start_vectors = jnp.transpose(start_vectors, (1, 0, 2))
    orb, nv, atoms = start_vectors.shape
    width = node_feat.shape[1]
    rows = 13 * PAD
    vec = nv * PAD

    def scratch(*shape, dtype=BF16):
        return pltpu.VMEM(shape, dtype)

    pair_blocks, filtered = pl.pallas_call(
        kernel,
        out_shape=(
            jax.ShapeDtypeStruct((w_out.shape[0], edges), BF16),
            jax.ShapeDtypeStruct(start_vectors.shape, F32),
        ),
        in_specs=[anywhere, anywhere, vmem, vmem, vmem] + [anywhere] * 6,
        out_specs=(anywhere, vmem),
        scratch_shapes=[
            scratch(atoms, width),
            scratch(atoms, width),
            scratch(CHIPS, edges, radial.shape[1]),
            scratch(*w_src.shape),
            scratch(*w_dst.shape),
            scratch(*w_radial.shape),
            scratch(*w_hidden.shape),
            scratch(*w_out.shape),
            scratch(*start_vectors.shape, dtype=F32),
            scratch(8, 8, 128, dtype=jnp.int32),
            scratch(8, 4 * atoms, edges),
            scratch(8, rows, edges),
            scratch(8, rows, edges, dtype=F32),
            scratch(8, nv, PAD, edges, dtype=F32),
            scratch(8, nv, PAD, edges, dtype=F32),
            scratch(CHIPS, width, edges, dtype=F32),
            scratch(vec, atoms),
            scratch(vec, atoms),
            scratch(3, width, 2 * atoms),
            scratch(*w_hidden.shape),
            scratch(width, radial.shape[1]),
            scratch(*w_dst.shape),
            scratch(rows, width),
            scratch(rows, rows),
            scratch(w_out.shape[0], edges),
        ]
        + [scratch(vec, atoms)] * 6
        + [
            pltpu.SemaphoreType.DMA((9,)),
            pltpu.SemaphoreType.DMA((17,)),
            pltpu.SemaphoreType.DMA((17,)),
        ],
        compiler_params=pltpu.CompilerParams(
            collective_id=0, has_side_effects=True, vmem_limit_bytes=60 * 1024 * 1024
        ),
        name="pair_filter",
    )(node_feat, radial, edge_src, edge_dst, edge_live, w_src, w_dst, w_radial, w_hidden, w_out, start_vectors)
    return pair_blocks, jnp.transpose(filtered, (1, 0, 2))


def solution(mesh):
    in_specs = (
        P("space", None),
        P(("space", "vec"), None),
        P(("space", "vec")),
        P(("space", "vec")),
        P(("space", "vec")),
        P(),
        P(),
        P(),
        P(),
        P(),
        P("vec", None, "space"),
    )
    out_specs = (P(None, ("space", "vec")), P("vec", None, "space"))
    return jax.shard_map(
        on_device, mesh=mesh, in_specs=in_specs, out_specs=out_specs, check_vma=False
    )
```

time: 56 us -> 41.8 us (0.75)
  the two profiles are of different devices: /device:TPU:1 before, /device:TPU:2 now
where the time goes in v2:
time: 41.8 us; the launch traced here: 41.6 us
  Pallas kernels  38.8 us (93%)
  local copies, waits for them, and re-layouts  2.15 us (5%)
  between operations  0.65 us (2%)
    pallas_call x1, Pallas kernels, on_device(): pl.pallas_call(kernel, out_shape=(jax.ShapeDtypeStruct((w_out.shape[0], e...  38.8 us
    unnamed x4, local copies, waits for them, and re-layouts  2.15 us

profile of v2, /device:TPU:2, one launch (start us, length us, event | category | flops | bytes accessed | tf_op | source)
XLA Modules:
  0.0 41.6 jit_solution(12079053873016095366)
XLA Ops:
  0.6 38.8 %pair_filter.1 = (bf16[169,256]{1,0:T(8,128)(2,1)}, f32[13,4,128]{2,1,0:T(4,128)}) custom-call(bf16[128,256]{1,0:T(8,128)(2,1)} %feat_hbm.1, bf16[256,128]{1,0:T(8,128)(2,1)} %radial_hbm.1, s32[256]{0:T(256)} %src_ref.1, s32[256]{0:T(256)} %dst_ref.1, s32[256]{0:T(256)} %live_ref.1, bf16[256,256]{1,0:T(8,128)(2,1)} %ws_hbm.1, bf16[256,256]{1,0:T(8,128)(2,1)} %wd_hbm.1, ...), custom_call_target="tpu_custom_call" | custom-call | tf_op jit(solution)/shard_map/pair_filter/pallas_call | solution.py:241
  39.5 0.0 copy-start
  39.5 1.5 %copy.15 = bf16[169,256]{1,0:T(8,128)(2,1)} copy(bf16[169,256]{1,0:T(8,128)(2,1)} %get-tuple-element.8) | data formatting | bytes 173056
  41.0 0.0 copy-done
  41.0 0.6 %copy.16 = f32[4,13,128]{2,0,1:T(4,128)} copy(f32[4,13,128]{2,0,1:T(4,128)S(1)} %bitcast.2) | data formatting | bytes 53248
Async XLA Ops:
  39.5 1.6 %copy-start = (f32[13,4,128]{2,1,0:T(4,128)S(1)}, f32[13,4,128]{2,1,0:T(4,128)}, u32[]{:S(2)}) copy-start(f32[13,4,128]{2,1,0:T(4,128)} %get-tuple-element.5) | copy-start | bytes 79876

commit v3 on v2

--- a/solution.py
+++ b/solution.py
@@ -31,39 +31,54 @@
 
 
 def kernel(
-    feat_hbm, radial_hbm, src_ref, dst_ref, live_ref, ws_hbm, wd_hbm, wr_hbm, wh_hbm, wo_hbm, sv_hbm,
-    blocks_hbm, out_ref,
+    feat_hbm, radial_hbm, src_hbm, dst_hbm, live_hbm, ws_hbm, wd_hbm, wr_hbm, wh_hbm, wo_hbm, sv_hbm,
+    blocks_ref, out_ref,
+    src_ref, dst_ref, live_ref,
     feat, ghost, rad, ws, wd, wr, wh, wo, sv,
     info, onehot, ha, hb, xs, xt, pre,
-    v_own, v_gh, proj, wht, wrt, wdt, wa, pb, blocks,
+    v_own, v_gh, proj, wht, wrt, wdt, wa, pb,
     gh_out, own_out, gh_in, own_in, gh2_out, gh2_in,
-    local_sem, send_sem, recv_sem,
+    local_sem, send_sem, recv_sem, ready_sem,
 ):
     n_space = lax.axis_size("space")
     d = lax.axis_index("space")
     j = lax.axis_index("vec")
     z, c = j // 2, j % 2
     zk = [z, z + 1 - 2 * (z % 2), (z + 2) % 4, 3 - z]
-    left = (lax.rem(d + n_space - 1, n_space), j)
-    right = (lax.rem(d + 1, n_space), j)
+    before, after = lax.rem(d + n_space - 1, n_space), lax.rem(d + 1, n_space)
+    left, right = (before, j), (after, j)
     same = [(d, zk[k] * 2 + c) for k in range(CHIPS)]
     sibling = (d, z * 2 + 1 - c)
+    feat_from = (after, (z + (d % 4) // 3 * (3 - 2 * z)) * 2 + 1)
+    feat_to = (before, (z + (before % 4) // 3 * (3 - 2 * z)) * 2 + 1)
     orb, nv = out_ref.shape[:2]
     layers = wh.shape[0]
 
-    partners = [left, right, sibling] + same[1:]
     barrier = pltpu.get_barrier_semaphore()
-    for dev in partners:
+
+    def hello(dev):
         pl.semaphore_signal(barrier, inc=1, device_id=dev, device_id_type=MESH)
+
+    @pl.when(c == 1)
+    def _():
+        hello(feat_from)
+        hello(sibling)
+
+    for nb in (after, before):
+        hello((nb, z * 2 + 1))
+    for k in range(1, CHIPS):
+        hello((d, zk[k] * 2))
 
     loads = []
     for i, (a, b) in enumerate(
-        [(sv_hbm, sv), (feat_hbm, feat), (ws_hbm, ws), (wd_hbm, wd), (wr_hbm, wr), (wh_hbm, wh), (wo_hbm, wo), (radial_hbm, rad.at[0])]
+        [(sv_hbm, sv), (feat_hbm, feat), (ws_hbm, ws), (wd_hbm, wd), (wr_hbm, wr), (wh_hbm, wh), (wo_hbm, wo), (radial_hbm, rad.at[0]), (src_hbm, src_ref), (dst_hbm, dst_ref), (live_hbm, live_ref)]
     ):
         cp = pltpu.make_async_copy(a, b, local_sem.at[i])
         cp.start()
         loads.append(cp)
 
+    for cp in loads[8:]:
+        cp.wait()
     for row, ref in enumerate((src_ref, dst_ref, live_ref)):
         for h in range(2):
             info[0, 2 * row + h : 2 * row + h + 1, :] = ref[h * 128 : (h + 1) * 128].reshape(1, 128)
@@ -74,24 +89,34 @@
     )
     v_own[...] = start.astype(BF16)
 
-    pl.semaphore_wait(barrier, len(partners))
+    def tell_other_core():
+        pl.semaphore_signal(ready_sem, inc=1, device_id=sibling, device_id_type=MESH)
+
+    @pl.when(c == 0)
+    def _():
+        pl.semaphore_wait(barrier, 7)
+        tell_other_core()
+
+    @pl.when(c == 1)
+    def _():
+        pl.semaphore_wait(ready_sem, 1)
 
     sent = []
 
-    def send(i, a, b, dev):
-        cp = pltpu.make_async_remote_copy(
+    def copy_to(i, a, b, dev):
+        return pltpu.make_async_remote_copy(
             src_ref=a, dst_ref=b, send_sem=send_sem.at[i], recv_sem=recv_sem.at[i],
             device_id=dev, device_id_type=MESH,
         )
+
+    def send(i, a, b, dev):
+        cp = copy_to(i, a, b, dev)
         cp.start()
         sent.append(cp)
         return cp
 
-    half = pl.ds(pl.multiple_of(c * 64, 64), 64)
-    half_in = send(0, feat_hbm.at[half, :], ghost.at[half, :], left)
-    vgh_in = send(1, v_own, v_gh, left)
-    info_in = [send(1 + k, info.at[0], info.at[k], same[k]) for k in (1, 2, 3)]
-    rad_in = [send(4 + k, radial_hbm, rad.at[k], same[k]) for k in (1, 3, 2)]
+    info_in = [send(k, info.at[0], info.at[k], same[k]) for k in (1, 2, 3)]
+    rad_in = [send(3 + k, radial_hbm, rad.at[k], same[k]) for k in (1, 3, 2)]
 
     def make_onehot(k, r):
         s, t = 2 * k + r, 4 * r + k
@@ -108,7 +133,7 @@
     for cp in info_in:
         cp.wait_recv()
     info_sib = send(8, info.at[0:4], info.at[4:8], sibling)
-    for cp in loads[1:]:
+    for cp in loads[1:8]:
         cp.wait()
 
     wdt[...] = transposed(wd[...])
@@ -135,8 +160,20 @@
     for k in range(1, CHIPS):
         make_onehot(k, 0)
 
-    half_in.wait_recv()
-    other_in = send(9, ghost.at[half, :], ghost.at[half, :], sibling)
+    feat_cp = copy_to(0, feat_hbm, ghost, feat_to)
+    pass_on = copy_to(9, ghost, ghost, sibling)
+
+    @pl.when(c == 1)
+    def _():
+        pl.semaphore_wait(barrier, 5)
+        feat_cp.start()
+        tell_other_core()
+
+    @pl.when(c == 0)
+    def _():
+        pl.semaphore_wait(ready_sem, 1)
+
+    vgh_in = send(7, v_own, v_gh, left)
 
     for cp in rad_in:
         cp.wait_recv()
@@ -148,7 +185,15 @@
     for k in range(CHIPS):
         make_onehot(k, 1)
 
-    other_in.wait_recv()
+    @pl.when(c == 1)
+    def _():
+        feat_cp.wait_recv()
+        pass_on.start()
+
+    @pl.when(c == 0)
+    def _():
+        pass_on.wait_recv()
+
     proj[2, :, 0:128], proj[2, :, 128:256] = halves(mm_nt(wdt[...], ghost[...]))
 
     every = range(CHIPS)
@@ -161,9 +206,7 @@
         ha[2 * k] = (mm(wa[...], hidden[k]) * live).astype(BF16)
         h_in.append(send(10 + k, ha.at[2 * k], ha.at[2 * k + 1], sibling))
         if k == 0:
-            blocks[...] = (mm(wo[...], hidden[0]) * live).astype(BF16)
-    blocks_out = pltpu.make_async_copy(blocks, blocks_hbm, local_sem.at[8])
-    blocks_out.start()
+            blocks_ref[...] = (mm(wo[...], hidden[0]) * live).astype(BF16)
 
     def to_targets(s, vec):
         xs[s] = mm(vec, onehot[s, 0:128, :]).reshape(nv, PAD, 256)
@@ -216,9 +259,14 @@
     for s in range(2 * CHIPS):
         p_s += to_sources(s, both1)
     second = 2.0 * (p_s + p_t[:, :128])
-    blocks_out.wait()
     for cp in sent:
         cp.wait_send()
+
+    @pl.when(c == 1)
+    def _():
+        feat_cp.wait_send()
+        pass_on.wait_send()
+
     gh2_in_cp.wait_recv()
     second = second + 2.0 * gh2_in[...].astype(F32)
     for v in range(nv):
@@ -241,12 +289,13 @@
     pair_blocks, filtered = pl.pallas_call(
         kernel,
         out_shape=(
-            jax.ShapeDtypeStruct((w_out.shape[0], edges), BF16),
-            jax.ShapeDtypeStruct(start_vectors.shape, F32),
+            pltpu.VMEM((w_out.shape[0], edges), BF16),
+            pltpu.VMEM(start_vectors.shape, F32),
         ),
-        in_specs=[anywhere, anywhere, vmem, vmem, vmem] + [anywhere] * 6,
-        out_specs=(anywhere, vmem),
-        scratch_shapes=[
+        in_specs=[anywhere] * 11,
+        out_specs=(vmem, vmem),
+        scratch_shapes=[scratch(edges, dtype=jnp.int32)] * 3
+        + [
             scratch(atoms, width),
             scratch(atoms, width),
             scratch(CHIPS, edges, radial.shape[1]),
@@ -271,13 +320,13 @@
             scratch(*w_dst.shape),
             scratch(rows, width),
             scratch(rows, rows),
-            scratch(w_out.shape[0], edges),
         ]
         + [scratch(vec, atoms)] * 6
         + [
-            pltpu.SemaphoreType.DMA((9,)),
+            pltpu.SemaphoreType.DMA((11,)),
             pltpu.SemaphoreType.DMA((17,)),
             pltpu.SemaphoreType.DMA((17,)),
+            pltpu.SemaphoreType.REGULAR,
         ],
         compiler_params=pltpu.CompilerParams(
             collective_id=0, has_side_effects=True, vmem_limit_bytes=60 * 1024 * 1024

time: 41.8 us -> 39 us (0.933)
  the two profiles are of different devices: /device:TPU:2 before, /device:TPU:1 now
where the time goes in v3:
time: 39 us; the launch traced here: 38.4 us
  Pallas kernels  36.6 us (94%)
  local copies, waits for them, and re-layouts  1.25 us (3%)
  between operations  0.64 us (2%)
    pallas_call x1, Pallas kernels, on_device(): pl.pallas_call(kernel, out_shape=(pltpu.VMEM((w_out.shape[0], edges), BF1...  36.6 us
    unnamed x2, local copies, waits for them, and re-layouts  1.25 us

profile of v3, /device:TPU:1, one launch (start us, length us, event | category | flops | bytes accessed | tf_op | source)
XLA Modules:
  0.0 38.4 jit_solution(6261869958619830792)
XLA Ops:
  0.6 36.6 %pair_filter.1 = (bf16[169,256]{1,0:T(8,128)(2,1)S(1)}, f32[13,4,128]{2,1,0:T(4,128)S(1)}) custom-call(bf16[128,256]{1,0:T(8,128)(2,1)} %feat_hbm.1, bf16[256,128]{1,0:T(8,128)(2,1)} %radial_hbm.1, s32[256]{0:T(256)} %src_hbm.1, s32[256]{0:T(256)} %dst_hbm.1, s32[256]{0:T(256)} %live_hbm.1, bf16[256,256]{1,0:T(8,128)(2,1)} %ws_hbm.1, ...), custom_call_target="tpu_custom_call" | custom-call | tf_op jit(solution)/shard_map/pair_filter/pallas_call | solution.py:289
  37.2 0.6 %copy.15 = bf16[169,256]{1,0:T(8,128)(2,1)} copy(bf16[169,256]{1,0:T(8,128)(2,1)S(1)} %get-tuple-element.6) | data formatting | bytes 173056
  37.8 0.6 %copy.16 = f32[4,13,128]{2,0,1:T(4,128)} copy(f32[4,13,128]{2,0,1:T(4,128)S(1)} %bitcast.2) | data formatting | bytes 53248

commit v4 on v3

--- a/solution.py
+++ b/solution.py
@@ -34,8 +34,8 @@
     feat_hbm, radial_hbm, src_hbm, dst_hbm, live_hbm, ws_hbm, wd_hbm, wr_hbm, wh_hbm, wo_hbm, sv_hbm,
     blocks_ref, out_ref,
     src_ref, dst_ref, live_ref,
-    feat, ghost, rad, ws, wd, wr, wh, wo, sv,
-    info, onehot, ha, hb, xs, xt, pre,
+    feat, ghost, via, rad, ws, wd, wr, wh, wo, sv,
+    info, onehot, ha, hf, hb, xs, xt, pre,
     v_own, v_gh, proj, wht, wrt, wdt, wa, pb,
     gh_out, own_out, gh_in, own_in, gh2_out, gh2_in,
     local_sem, send_sem, recv_sem, ready_sem,
@@ -49,8 +49,10 @@
     left, right = (before, j), (after, j)
     same = [(d, zk[k] * 2 + c) for k in range(CHIPS)]
     sibling = (d, z * 2 + 1 - c)
-    feat_from = (after, (z + (d % 4) // 3 * (3 - 2 * z)) * 2 + 1)
-    feat_to = (before, (z + (before % 4) // 3 * (3 - 2 * z)) * 2 + 1)
+    at_end, at_start = d % 4 == 3, d % 4 == 0
+    flip = d + 4 - 8 * (d // 4 % 2)
+    flip_before = before + 4 - 8 * (before // 4 % 2)
+    flip_after = lax.rem(flip + 1, n_space)
     orb, nv = out_ref.shape[:2]
     layers = wh.shape[0]
 
@@ -59,15 +61,23 @@
     def hello(dev):
         pl.semaphore_signal(barrier, inc=1, device_id=dev, device_id_type=MESH)
 
-    @pl.when(c == 1)
-    def _():
-        hello(feat_from)
-        hello(sibling)
+    @pl.when((c == 1) & at_end)
+    def _():
+        hello((flip, (3 - z) * 2))
+        hello((flip_after, z * 2))
+
+    @pl.when((c == 1) & jnp.logical_not(at_end))
+    def _():
+        hello((after, z * 2))
 
     for nb in (after, before):
         hello((nb, z * 2 + 1))
     for k in range(1, CHIPS):
         hello((d, zk[k] * 2))
+
+    @pl.when(c == 1)
+    def _():
+        hello(sibling)
 
     loads = []
     for i, (a, b) in enumerate(
@@ -77,7 +87,7 @@
         cp.start()
         loads.append(cp)
 
-    for cp in loads[8:]:
+    for cp in loads[7:] + loads[1:2]:
         cp.wait()
     for row, ref in enumerate((src_ref, dst_ref, live_ref)):
         for h in range(2):
@@ -94,7 +104,14 @@
 
     @pl.when(c == 0)
     def _():
-        pl.semaphore_wait(barrier, 7)
+        @pl.when(at_end)
+        def _():
+            pl.semaphore_wait(barrier, 9)
+
+        @pl.when(jnp.logical_not(at_end))
+        def _():
+            pl.semaphore_wait(barrier, 8)
+
         tell_other_core()
 
     @pl.when(c == 1)
@@ -103,9 +120,9 @@
 
     sent = []
 
-    def copy_to(i, a, b, dev):
+    def copy_to(i, a, b, dev, own=None):
         return pltpu.make_async_remote_copy(
-            src_ref=a, dst_ref=b, send_sem=send_sem.at[i], recv_sem=recv_sem.at[i],
+            src_ref=a, dst_ref=b, send_sem=send_sem.at[i if own is None else own], recv_sem=recv_sem.at[i],
             device_id=dev, device_id_type=MESH,
         )
 
@@ -116,7 +133,25 @@
         return cp
 
     info_in = [send(k, info.at[0], info.at[k], same[k]) for k in (1, 2, 3)]
-    rad_in = [send(3 + k, radial_hbm, rad.at[k], same[k]) for k in (1, 3, 2)]
+    feat_near = copy_to(0, feat, ghost, (before, z * 2 + 1))
+    feat_far = copy_to(17, feat, via, (flip_before, z * 2 + 1))
+    feat_via = copy_to(0, via, ghost, (flip, (3 - z) * 2 + 1), 18)
+    pass_on = copy_to(9, ghost, ghost, sibling)
+
+    @pl.when((c == 1) & at_start)
+    def _():
+        feat_far.start()
+
+    @pl.when((c == 1) & jnp.logical_not(at_start))
+    def _():
+        feat_near.start()
+
+    rad_in = [send(3 + k, rad.at[0], rad.at[k], same[k]) for k in (1, 3, 2)]
+
+    @pl.when((c == 1) & at_end & (flip > d))
+    def _():
+        feat_far.wait_recv()
+        feat_via.start()
 
     def make_onehot(k, r):
         s, t = 2 * k + r, 4 * r + k
@@ -133,7 +168,7 @@
     for cp in info_in:
         cp.wait_recv()
     info_sib = send(8, info.at[0:4], info.at[4:8], sibling)
-    for cp in loads[1:8]:
+    for cp in loads[2:7]:
         cp.wait()
 
     wdt[...] = transposed(wd[...])
@@ -160,13 +195,9 @@
     for k in range(1, CHIPS):
         make_onehot(k, 0)
 
-    feat_cp = copy_to(0, feat_hbm, ghost, feat_to)
-    pass_on = copy_to(9, ghost, ghost, sibling)
-
     @pl.when(c == 1)
     def _():
-        pl.semaphore_wait(barrier, 5)
-        feat_cp.start()
+        pl.semaphore_wait(barrier, 4)
         tell_other_core()
 
     @pl.when(c == 0)
@@ -175,19 +206,25 @@
 
     vgh_in = send(7, v_own, v_gh, left)
 
-    for cp in rad_in:
-        cp.wait_recv()
+    @pl.when((c == 1) & at_end & (flip < d))
+    def _():
+        feat_far.wait_recv()
+        feat_via.start()
+
+    info_sib.wait_recv()
     for k in range(CHIPS):
+        make_onehot(k, 1)
+    arrived = dict(zip((1, 3, 2), rad_in))
+    for k in (0, 1, 3, 2):
+        if k:
+            arrived[k].wait_recv()
         pre[k] = (
             mm(proj[0], onehot[2 * k, 0:256, :]) + mm(proj[1], onehot[2 * k, 0:256, :]) + mm_nt(wrt[...], rad[k])
         )
-    info_sib.wait_recv()
-    for k in range(CHIPS):
-        make_onehot(k, 1)
 
     @pl.when(c == 1)
     def _():
-        feat_cp.wait_recv()
+        feat_near.wait_recv()
         pass_on.start()
 
     @pl.when(c == 0)
@@ -208,11 +245,11 @@
         if k == 0:
             blocks_ref[...] = (mm(wo[...], hidden[0]) * live).astype(BF16)
 
-    def to_targets(s, vec):
+    def to_targets(s, vec, h):
         xs[s] = mm(vec, onehot[s, 0:128, :]).reshape(nv, PAD, 256)
         acc = jnp.zeros((nv, PAD, 256), F32)
         for a in range(orb):
-            acc += ha[s, a * PAD : (a + 1) * PAD, :].astype(F32)[None] * xs[s, :, a : a + 1, :]
+            acc += h[s, a * PAD : (a + 1) * PAD, :].astype(F32)[None] * xs[s, :, a : a + 1, :]
         return mm_nt(acc.reshape(nv * PAD, 256).astype(BF16), onehot[s, 128:384, :])
 
     def to_sources(s, vec):
@@ -222,34 +259,34 @@
             acc += hb[s, b * PAD : (b + 1) * PAD, :][None] * xt[s, :, b : b + 1, :]
         return mm_nt(acc.reshape(nv * PAD, 256).astype(BF16), onehot[s, 0:128, :])
 
-    vgh_in.wait_recv()
     own = v_own[...]
-    both = jnp.concatenate([own, v_gh[...]], 1)
     p_t = jnp.zeros((nv * PAD, 256), F32)
     p_s = jnp.zeros((nv * PAD, 128), F32)
     for s in range(0, 2 * CHIPS, 2):
-        hb[s] = mm(pb[...], ha[s])
-        p_t += to_targets(s, own)
-        p_s += to_sources(s, both)
+        p_t += to_targets(s, own, ha)
     for cp in h_in:
         cp.wait_recv()
     for s in range(1, 2 * CHIPS, 2):
-        p_t += to_targets(s, own)
+        p_t += to_targets(s, own, ha)
     part_gh = p_t[:, 128:]
     gh_out[...] = part_gh.astype(BF16)
     gh_in_cp = send(14, gh_out, gh_in, right)
-    for s in range(1, 2 * CHIPS, 2):
+    vgh_in.wait_recv()
+    both = jnp.concatenate([own, v_gh[...]], 1)
+    for s in range(2 * CHIPS):
         hb[s] = mm(pb[...], ha[s])
         p_s += to_sources(s, both)
     part_own = p_s + p_t[:, :128]
     own_out[...] = part_own.astype(BF16)
     own_in_cp = send(15, own_out, own_in, left)
 
+    for s in range(2 * CHIPS):
+        hf[s] = ha[s].astype(F32)
     gh_in_cp.wait_recv()
     own1 = (part_own + gh_in[...].astype(F32)).astype(BF16)
     p_t = jnp.zeros((nv * PAD, 256), F32)
     for s in range(2 * CHIPS):
-        p_t += to_targets(s, own1)
+        p_t += to_targets(s, own1, hf)
     gh2_out[...] = p_t[:, 128:].astype(BF16)
     gh2_in_cp = send(16, gh2_out, gh2_in, right)
     own_in_cp.wait_recv()
@@ -264,8 +301,19 @@
 
     @pl.when(c == 1)
     def _():
-        feat_cp.wait_send()
         pass_on.wait_send()
+
+    @pl.when((c == 1) & at_start)
+    def _():
+        feat_far.wait_send()
+
+    @pl.when((c == 1) & jnp.logical_not(at_start))
+    def _():
+        feat_near.wait_send()
+
+    @pl.when((c == 1) & at_end)
+    def _():
+        feat_via.wait_send()
 
     gh2_in_cp.wait_recv()
     second = second + 2.0 * gh2_in[...].astype(F32)
@@ -298,6 +346,7 @@
         + [
             scratch(atoms, width),
             scratch(atoms, width),
+            scratch(atoms, width),
             scratch(CHIPS, edges, radial.shape[1]),
             scratch(*w_src.shape),
             scratch(*w_dst.shape),
@@ -308,6 +357,7 @@
             scratch(8, 8, 128, dtype=jnp.int32),
             scratch(8, 4 * atoms, edges),
             scratch(8, rows, edges),
+            scratch(8, rows, edges, dtype=F32),
             scratch(8, rows, edges, dtype=F32),
             scratch(8, nv, PAD, edges, dtype=F32),
             scratch(8, nv, PAD, edges, dtype=F32),
@@ -324,8 +374,8 @@
         + [scratch(vec, atoms)] * 6
         + [
             pltpu.SemaphoreType.DMA((11,)),
-            pltpu.SemaphoreType.DMA((17,)),
-            pltpu.SemaphoreType.DMA((17,)),
+            pltpu.SemaphoreType.DMA((19,)),
+            pltpu.SemaphoreType.DMA((19,)),
             pltpu.SemaphoreType.REGULAR,
         ],
         compiler_params=pltpu.CompilerParams(

time: 39 us -> 37.7 us (0.967); the launches traced: 38.4 us -> 37.6 us
  Pallas kernels: 36.6 us -> 35.7 us
    pallas_call x1, Pallas kernels: 36.6 us -> 35.7 us  [on_device(): pl.pallas_call(kernel, out_shape=(pltpu.VMEM((w_out.shape[0], edges), BF1...]
where the time goes in v4:
time: 37.7 us; the launch traced here: 37.6 us
  Pallas kernels  35.7 us (95%)
  local copies, waits for them, and re-layouts  1.25 us (3%)
  between operations  0.64 us (2%)
    pallas_call x1, Pallas kernels, on_device(): pl.pallas_call(kernel, out_shape=(pltpu.VMEM((w_out.shape[0], edges), BF1...  35.7 us
    unnamed x2, local copies, waits for them, and re-layouts  1.25 us

profile of v4, /device:TPU:1, one launch (start us, length us, event | category | flops | bytes accessed | tf_op | source)
XLA Modules:
  0.0 37.6 jit_solution(301273130648570837)
XLA Ops:
  0.6 35.7 %pair_filter.1 = (bf16[169,256]{1,0:T(8,128)(2,1)S(1)}, f32[13,4,128]{2,1,0:T(4,128)S(1)}) custom-call(bf16[128,256]{1,0:T(8,128)(2,1)} %feat_hbm.1, bf16[256,128]{1,0:T(8,128)(2,1)} %radial_hbm.1, s32[256]{0:T(256)} %src_hbm.1, s32[256]{0:T(256)} %dst_hbm.1, s32[256]{0:T(256)} %live_hbm.1, bf16[256,256]{1,0:T(8,128)(2,1)} %ws_hbm.1, ...), custom_call_target="tpu_custom_call" | custom-call | tf_op jit(solution)/shard_map/pair_filter/pallas_call | solution.py:337
  36.4 0.6 %copy.15 = bf16[169,256]{1,0:T(8,128)(2,1)} copy(bf16[169,256]{1,0:T(8,128)(2,1)S(1)} %get-tuple-element.6) | data formatting | bytes 173056
  37.0 0.6 %copy.16 = f32[4,13,128]{2,0,1:T(4,128)} copy(f32[4,13,128]{2,0,1:T(4,128)S(1)} %bitcast.2) | data formatting | bytes 53248

commit v5 on v4

--- a/solution.py
+++ b/solution.py
@@ -35,7 +35,7 @@
     blocks_ref, out_ref,
     src_ref, dst_ref, live_ref,
     feat, ghost, via, rad, ws, wd, wr, wh, wo, sv,
-    info, onehot, ha, hf, hb, xs, xt, pre,
+    info, onehot, ha, hf, hb, xs, xt,
     v_own, v_gh, proj, wht, wrt, wdt, wa, pb,
     gh_out, own_out, gh_in, own_in, gh2_out, gh2_in,
     local_sem, send_sem, recv_sem, ready_sem,
@@ -214,14 +214,6 @@
     info_sib.wait_recv()
     for k in range(CHIPS):
         make_onehot(k, 1)
-    arrived = dict(zip((1, 3, 2), rad_in))
-    for k in (0, 1, 3, 2):
-        if k:
-            arrived[k].wait_recv()
-        pre[k] = (
-            mm(proj[0], onehot[2 * k, 0:256, :]) + mm(proj[1], onehot[2 * k, 0:256, :]) + mm_nt(wrt[...], rad[k])
-        )
-
     @pl.when(c == 1)
     def _():
         feat_near.wait_recv()
@@ -233,17 +225,25 @@
 
     proj[2, :, 0:128], proj[2, :, 128:256] = halves(mm_nt(wdt[...], ghost[...]))
 
-    every = range(CHIPS)
-    hidden = [silu(pre[k] + mm(proj[2], onehot[2 * k, 256:512, :])).astype(BF16) for k in every]
-    for layer in range(layers):
-        hidden = [(hidden[k].astype(F32) + silu(mm(wht[layer], hidden[k]))).astype(BF16) for k in every]
+    arrived = dict(zip((1, 3, 2), rad_in))
     h_in = []
-    for k in every:
-        live = jnp.concatenate([info[k, 4:5, :], info[k, 5:6, :]], 1).astype(F32)
-        ha[2 * k] = (mm(wa[...], hidden[k]) * live).astype(BF16)
-        h_in.append(send(10 + k, ha.at[2 * k], ha.at[2 * k + 1], sibling))
-        if k == 0:
-            blocks_ref[...] = (mm(wo[...], hidden[0]) * live).astype(BF16)
+    for batch in ((0, 1, 3), (2,)):
+        for k in batch:
+            if k:
+                arrived[k].wait_recv()
+        pre = [
+            mm(proj[0], onehot[2 * k, 0:256, :]) + mm(proj[1], onehot[2 * k, 0:256, :]) + mm_nt(wrt[...], rad[k])
+            for k in batch
+        ]
+        hidden = [silu(p + mm(proj[2], onehot[2 * k, 256:512, :])).astype(BF16) for p, k in zip(pre, batch)]
+        for layer in range(layers):
+            hidden = [(h.astype(F32) + silu(mm(wht[layer], h))).astype(BF16) for h in hidden]
+        for h, k in zip(hidden, batch):
+            live = jnp.concatenate([info[k, 4:5, :], info[k, 5:6, :]], 1).astype(F32)
+            ha[2 * k] = (mm(wa[...], h) * live).astype(BF16)
+            h_in.append(send(10 + k, ha.at[2 * k], ha.at[2 * k + 1], sibling))
+            if k == 0:
+                blocks_ref[...] = (mm(wo[...], h) * live).astype(BF16)
 
     def to_targets(s, vec, h):
         xs[s] = mm(vec, onehot[s, 0:128, :]).reshape(nv, PAD, 256)
@@ -361,7 +361,6 @@
             scratch(8, rows, edges, dtype=F32),
             scratch(8, nv, PAD, edges, dtype=F32),
             scratch(8, nv, PAD, edges, dtype=F32),
-            scratch(CHIPS, width, edges, dtype=F32),
             scratch(vec, atoms),
             scratch(vec, atoms),
             scratch(3, width, 2 * atoms),

time: 37.7 us -> 36.1 us (0.958)
  Pallas kernels: 35.7 us -> 34 us
    pallas_call x1, Pallas kernels: 35.7 us -> 34 us  [on_device(): pl.pallas_call(kernel, out_shape=(pltpu.VMEM((w_out.shape[0], edges), BF1...]
where the time goes in v5:
time: 36.1 us; the launch traced here: 35.9 us
  Pallas kernels  34 us (94%)
  local copies, waits for them, and re-layouts  1.25 us (3%)
  between operations  0.64 us (2%)
    pallas_call x1, Pallas kernels, on_device(): pl.pallas_call(kernel, out_shape=(pltpu.VMEM((w_out.shape[0], edges), BF1...  34 us
    unnamed x2, local copies, waits for them, and re-layouts  1.25 us

profile of v5, /device:TPU:1, one launch (start us, length us, event | category | flops | bytes accessed | tf_op | source)
XLA Modules:
  0.0 35.9 jit_solution(3194254330691274468)
XLA Ops:
  0.6 34.0 %pair_filter.1 = (bf16[169,256]{1,0:T(8,128)(2,1)S(1)}, f32[13,4,128]{2,1,0:T(4,128)S(1)}) custom-call(bf16[128,256]{1,0:T(8,128)(2,1)} %feat_hbm.1, bf16[256,128]{1,0:T(8,128)(2,1)} %radial_hbm.1, s32[256]{0:T(256)} %src_hbm.1, s32[256]{0:T(256)} %dst_hbm.1, s32[256]{0:T(256)} %live_hbm.1, bf16[256,256]{1,0:T(8,128)(2,1)} %ws_hbm.1, ...), custom_call_target="tpu_custom_call" | custom-call | tf_op jit(solution)/shard_map/pair_filter/pallas_call | solution.py:337
  34.7 0.6 %copy.15 = bf16[169,256]{1,0:T(8,128)(2,1)} copy(bf16[169,256]{1,0:T(8,128)(2,1)S(1)} %get-tuple-element.6) | data formatting | bytes 173056
  35.3 0.6 %copy.16 = f32[4,13,128]{2,0,1:T(4,128)} copy(f32[4,13,128]{2,0,1:T(4,128)S(1)} %bitcast.2) | data formatting | bytes 53248

commit v6 on v5

--- a/solution.py
+++ b/solution.py
@@ -63,19 +63,19 @@
 
     @pl.when((c == 1) & at_end)
     def _():
-        hello((flip, (3 - z) * 2))
-        hello((flip_after, z * 2))
+        hello((flip, (3 - z) * 2 + 1))
+        hello((flip_after, z * 2 + 1))
 
     @pl.when((c == 1) & jnp.logical_not(at_end))
     def _():
-        hello((after, z * 2))
+        hello((after, z * 2 + 1))
 
     for nb in (after, before):
-        hello((nb, z * 2 + 1))
+        hello((nb, z * 2))
     for k in range(1, CHIPS):
-        hello((d, zk[k] * 2))
-
-    @pl.when(c == 1)
+        hello((d, zk[k] * 2 + 1))
+
+    @pl.when(c == 0)
     def _():
         hello(sibling)
 
@@ -102,7 +102,7 @@
     def tell_other_core():
         pl.semaphore_signal(ready_sem, inc=1, device_id=sibling, device_id_type=MESH)
 
-    @pl.when(c == 0)
+    @pl.when(c == 1)
     def _():
         @pl.when(at_end)
         def _():
@@ -114,7 +114,7 @@
 
         tell_other_core()
 
-    @pl.when(c == 1)
+    @pl.when(c == 0)
     def _():
         pl.semaphore_wait(ready_sem, 1)
 
@@ -195,12 +195,12 @@
     for k in range(1, CHIPS):
         make_onehot(k, 0)
 
-    @pl.when(c == 1)
+    @pl.when(c == 0)
     def _():
         pl.semaphore_wait(barrier, 4)
         tell_other_core()
 
-    @pl.when(c == 0)
+    @pl.when(c == 1)
     def _():
         pl.semaphore_wait(ready_sem, 1)
 
@@ -226,7 +226,7 @@
     proj[2, :, 0:128], proj[2, :, 128:256] = halves(mm_nt(wdt[...], ghost[...]))
 
     arrived = dict(zip((1, 3, 2), rad_in))
-    h_in = []
+    h_in = {}
     for batch in ((0, 1, 3), (2,)):
         for k in batch:
             if k:
@@ -241,7 +241,7 @@
         for h, k in zip(hidden, batch):
             live = jnp.concatenate([info[k, 4:5, :], info[k, 5:6, :]], 1).astype(F32)
             ha[2 * k] = (mm(wa[...], h) * live).astype(BF16)
-            h_in.append(send(10 + k, ha.at[2 * k], ha.at[2 * k + 1], sibling))
+            h_in[k] = send(10 + k, ha.at[2 * k], ha.at[2 * k + 1], sibling)
             if k == 0:
                 blocks_ref[...] = (mm(wo[...], h) * live).astype(BF16)
 
@@ -262,12 +262,14 @@
     own = v_own[...]
     p_t = jnp.zeros((nv * PAD, 256), F32)
     p_s = jnp.zeros((nv * PAD, 128), F32)
-    for s in range(0, 2 * CHIPS, 2):
-        p_t += to_targets(s, own, ha)
-    for cp in h_in:
-        cp.wait_recv()
-    for s in range(1, 2 * CHIPS, 2):
-        p_t += to_targets(s, own, ha)
+    for k in range(CHIPS):
+        p_t += to_targets(2 * k, own, ha)
+    for k in (0, 1, 3):
+        h_in[k].wait_recv()
+    for k in (0, 1, 3):
+        p_t += to_targets(2 * k + 1, own, ha)
+    h_in[2].wait_recv()
+    p_t += to_targets(5, own, ha)
     part_gh = p_t[:, 128:]
     gh_out[...] = part_gh.astype(BF16)
     gh_in_cp = send(14, gh_out, gh_in, right)

time: 36.1 us -> 35.5 us (0.983)
  Pallas kernels: 34 us -> 33.4 us
    pallas_call x1, Pallas kernels: 34 us -> 33.4 us  [on_device(): pl.pallas_call(kernel, out_shape=(pltpu.VMEM((w_out.shape[0], edges), BF1...]
where the time goes in v6:
time: 35.5 us; the launch traced here: 35.3 us
  Pallas kernels  33.4 us (94%)
  local copies, waits for them, and re-layouts  1.25 us (4%)
  between operations  0.64 us (2%)
    pallas_call x1, Pallas kernels, on_device(): pl.pallas_call(kernel, out_shape=(pltpu.VMEM((w_out.shape[0], edges), BF1...  33.4 us
    unnamed x2, local copies, waits for them, and re-layouts  1.25 us

profile of v6, /device:TPU:1, one launch (start us, length us, event | category | flops | bytes accessed | tf_op | source)
XLA Modules:
  0.0 35.3 jit_solution(10253120766335111885)
XLA Ops:
  0.6 33.4 %pair_filter.1 = (bf16[169,256]{1,0:T(8,128)(2,1)S(1)}, f32[13,4,128]{2,1,0:T(4,128)S(1)}) custom-call(bf16[128,256]{1,0:T(8,128)(2,1)} %feat_hbm.1, bf16[256,128]{1,0:T(8,128)(2,1)} %radial_hbm.1, s32[256]{0:T(256)} %src_hbm.1, s32[256]{0:T(256)} %dst_hbm.1, s32[256]{0:T(256)} %live_hbm.1, bf16[256,256]{1,0:T(8,128)(2,1)} %ws_hbm.1, ...), custom_call_target="tpu_custom_call" | custom-call | tf_op jit(solution)/shard_map/pair_filter/pallas_call | solution.py:339
  34.1 0.6 %copy.15 = bf16[169,256]{1,0:T(8,128)(2,1)} copy(bf16[169,256]{1,0:T(8,128)(2,1)S(1)} %get-tuple-element.6) | data formatting | bytes 173056
  34.7 0.6 %copy.16 = f32[4,13,128]{2,0,1:T(4,128)} copy(f32[4,13,128]{2,0,1:T(4,128)S(1)} %bitcast.2) | data formatting | bytes 53248

commit v7 on v6

--- a/solution.py
+++ b/solution.py
@@ -35,7 +35,7 @@
     blocks_ref, out_ref,
     src_ref, dst_ref, live_ref,
     feat, ghost, via, rad, ws, wd, wr, wh, wo, sv,
-    info, onehot, ha, hf, hb, xs, xt,
+    info, onehot, ha, hf, hb, xs, xt, ys,
     v_own, v_gh, proj, wht, wrt, wdt, wa, pb,
     gh_out, own_out, gh_in, own_in, gh2_out, gh2_in,
     local_sem, send_sem, recv_sem, ready_sem,
@@ -245,12 +245,15 @@
             if k == 0:
                 blocks_ref[...] = (mm(wo[...], h) * live).astype(BF16)
 
-    def to_targets(s, vec, h):
+    def target_products(s, vec, h):
         xs[s] = mm(vec, onehot[s, 0:128, :]).reshape(nv, PAD, 256)
         acc = jnp.zeros((nv, PAD, 256), F32)
         for a in range(orb):
             acc += h[s, a * PAD : (a + 1) * PAD, :].astype(F32)[None] * xs[s, :, a : a + 1, :]
-        return mm_nt(acc.reshape(nv * PAD, 256).astype(BF16), onehot[s, 128:384, :])
+        return acc.reshape(nv * PAD, 256).astype(BF16)
+
+    def to_targets(s, vec, h):
+        return mm_nt(target_products(s, vec, h), onehot[s, 128:384, :])
 
     def to_sources(s, vec):
         xt[s] = mm(vec, onehot[s, 128:384, :]).reshape(nv, PAD, 256)
@@ -286,18 +289,19 @@
         hf[s] = ha[s].astype(F32)
     gh_in_cp.wait_recv()
     own1 = (part_own + gh_in[...].astype(F32)).astype(BF16)
-    p_t = jnp.zeros((nv * PAD, 256), F32)
+    p_g = jnp.zeros((nv * PAD, 128), F32)
     for s in range(2 * CHIPS):
-        p_t += to_targets(s, own1, hf)
-    gh2_out[...] = p_t[:, 128:].astype(BF16)
+        ys[s] = target_products(s, own1, hf)
+        p_g += mm_nt(ys[s], onehot[s, 256:384, :])
+    gh2_out[...] = p_g.astype(BF16)
     gh2_in_cp = send(16, gh2_out, gh2_in, right)
     own_in_cp.wait_recv()
     gh1 = (part_gh + own_in[...].astype(F32)).astype(BF16)
     both1 = jnp.concatenate([own1, gh1], 1)
     p_s = jnp.zeros((nv * PAD, 128), F32)
     for s in range(2 * CHIPS):
-        p_s += to_sources(s, both1)
-    second = 2.0 * (p_s + p_t[:, :128])
+        p_s += mm_nt(ys[s], onehot[s, 128:256, :]) + to_sources(s, both1)
+    second = 2.0 * p_s
     for cp in sent:
         cp.wait_send()
 
@@ -363,6 +367,7 @@
             scratch(8, rows, edges, dtype=F32),
             scratch(8, nv, PAD, edges, dtype=F32),
             scratch(8, nv, PAD, edges, dtype=F32),
+            scratch(8, vec, edges),
             scratch(vec, atoms),
             scratch(vec, atoms),
             scratch(3, width, 2 * atoms),

time: 35.5 us -> 35.3 us (level)
  no operation moved by 1% of the time
where the time goes in v7:
time: 35.3 us; the launch traced here: 35.2 us
  Pallas kernels  33.3 us (94%)
  local copies, waits for them, and re-layouts  1.25 us (4%)
  between operations  0.64 us (2%)
    pallas_call x1, Pallas kernels, on_device(): pl.pallas_call(kernel, out_shape=(pltpu.VMEM((w_out.shape[0], edges), BF1...  33.3 us
    unnamed x2, local copies, waits for them, and re-layouts  1.25 us

profile of v7, /device:TPU:1, one launch (start us, length us, event | category | flops | bytes accessed | tf_op | source)
XLA Modules:
  0.0 35.2 jit_solution(627765556901947915)
XLA Ops:
  0.6 33.3 %pair_filter.1 = (bf16[169,256]{1,0:T(8,128)(2,1)S(1)}, f32[13,4,128]{2,1,0:T(4,128)S(1)}) custom-call(bf16[128,256]{1,0:T(8,128)(2,1)} %feat_hbm.1, bf16[256,128]{1,0:T(8,128)(2,1)} %radial_hbm.1, s32[256]{0:T(256)} %src_hbm.1, s32[256]{0:T(256)} %dst_hbm.1, s32[256]{0:T(256)} %live_hbm.1, bf16[256,256]{1,0:T(8,128)(2,1)} %ws_hbm.1, ...), custom_call_target="tpu_custom_call" | custom-call | tf_op jit(solution)/shard_map/pair_filter/pallas_call | solution.py:343
  34.0 0.6 %copy.15 = bf16[169,256]{1,0:T(8,128)(2,1)} copy(bf16[169,256]{1,0:T(8,128)(2,1)S(1)} %get-tuple-element.6) | data formatting | bytes 173056
  34.6 0.6 %copy.16 = f32[4,13,128]{2,0,1:T(4,128)} copy(f32[4,13,128]{2,0,1:T(4,128)S(1)} %bitcast.2) | data formatting | bytes 53248
